TPU v7x, 32 devices: a whole 2x2x4 slice. The times are simulated.
32 devices in a mesh: dp: 4 (over z), ctx: 2 (over y), tp: 4 (over x, core).
Axes of the slice: x: 2, y: 2, z: 4, core: 2. Of those that a mesh axis runs over, the one named last changes fastest.
Arguments:
- tokens: bfloat16 [8, 2048, 1024], P('dp', 'ctx'), may hold values from -6 to 6
- lengths: int32 [8, 4], P('dp'), may hold values from 1 to 1025, 2048 in all within a row
- w_q: bfloat16 [1024, 1024], P(('dp', 'ctx'), 'tp'), may hold values from -0.1875 to 0.1875
- w_k: bfloat16 [1024, 1024], P(('dp', 'ctx'), 'tp'), may hold values from -0.1875 to 0.1875
- w_v: bfloat16 [1024, 2048], P(('dp', 'ctx'), 'tp'), may hold values from -0.1875 to 0.1875
- w_g: bfloat16 [1024, 2048], P(('dp', 'ctx'), 'tp'), may hold values from -0.1875 to 0.1875
- w_a: bfloat16 [1024, 8], P(('dp', 'ctx'), 'tp'), may hold values from -0.1875 to 0.1875
- w_b: bfloat16 [1024, 8], P(('dp', 'ctx'), 'tp'), may hold values from -0.1875 to 0.1875
- output_weight: bfloat16 [1024, 2048], P(('dp', 'ctx'), 'tp'), may hold values from -0.1875 to 0.1875
- w_gate: bfloat16 [1024, 2816], P(('dp', 'ctx'), 'tp'), may hold values from -0.1875 to 0.1875
- w_up: bfloat16 [1024, 2816], P(('dp', 'ctx'), 'tp'), may hold values from -0.1875 to 0.1875
- w_down: bfloat16 [1024, 2816], P(('dp', 'ctx'), 'tp'), may hold values from -0.15625 to 0.15625
- gain_attn: bfloat16 [1024], P(('dp', 'ctx')), may hold values from 0.5 to 1.5
- gain_ffn: bfloat16 [1024], P(('dp', 'ctx')), may hold values from 0.5 to 1.5
- gain_out: bfloat16 [256], P(('dp', 'ctx')), may hold values from 0.5 to 1.5
- conv_q: bfloat16 [4, 1024], P(None, 'tp'), may hold values from -3 to 3
- conv_k: bfloat16 [4, 1024], P(None, 'tp'), may hold values from -3 to 3
- conv_v: bfloat16 [4, 2048], P(None, 'tp'), may hold values from -3 to 3
- a_log: float32 [8], P('tp'), may hold values from 0 to 2.7
- dt_bias: float32 [8], P('tp'), may hold values from -8 to -3
- d_out: bfloat16 [8, 2048, 1024], P('dp', 'ctx'), may hold values from -6 to 6
Outputs:
- layer_out: bfloat16 [8, 2048, 1024], P('dp', 'ctx')
- grad_tokens: float32 [8, 2048, 1024], P('dp', 'ctx')
- grad_w_q: float32 [1024, 1024], P(('dp', 'ctx'), 'tp')
- grad_w_k: float32 [1024, 1024], P(('dp', 'ctx'), 'tp')
- grad_w_v: float32 [1024, 2048], P(('dp', 'ctx'), 'tp')
- grad_w_g: float32 [1024, 2048], P(('dp', 'ctx'), 'tp')
- grad_w_a: float32 [1024, 8], P(('dp', 'ctx'), 'tp')
- grad_w_b: float32 [1024, 8], P(('dp', 'ctx'), 'tp')
- grad_w_o: float32 [1024, 2048], P(('dp', 'ctx'), 'tp')
- grad_w_gate: float32 [1024, 2816], P(('dp', 'ctx'), 'tp')
- grad_w_up: float32 [1024, 2816], P(('dp', 'ctx'), 'tp')
- grad_w_down: float32 [1024, 2816], P(('dp', 'ctx'), 'tp')
- grad_gain_attn: float32 [1024], P(('dp', 'ctx'))
- grad_gain_ffn: float32 [1024], P(('dp', 'ctx'))
- grad_gain_out: float32 [256], P(('dp', 'ctx'))
- grad_conv_q: float32 [4, 1024], P(None, 'tp')
- grad_conv_k: float32 [4, 1024], P(None, 'tp')
- grad_conv_v: float32 [4, 2048], P(None, 'tp')
- grad_a_log: float32 [8], P('tp')
- grad_dt_bias: float32 [8], P('tp')
Inputs may be any that keep to these rules, and one draw needn't show every extreme that they name: In each stream the 4 lengths sum to 2048, and one of them is exactly 1025.
All inputs are finite; a program needn't handle non-finite values.
Results may differ from a plain program's by a relative error of at most 0.014.
Values may be sent and summed in bfloat16 or wider, within the bound.
A program may use at most 320 MiB of HBM per device.

v0:
```python
from functools import partial

import jax
import jax.numpy as jnp
from jax import lax
from jax.sharding import PartitionSpec as P

BLOCK = 64


highest_precision = lax.Precision.HIGHEST
norm_epsilon = 1e-05
unit_epsilon = 1e-06


def from_behind(value, axis, steps):
    count = lax.axis_size(axis)
    leading, last = (max(0, -steps), min(count, count - steps))
    return lax.ppermute(value, axis, [(source, source + steps) for source in range(leading, last)])


def prefix(array, axis, combine, identity):
    length, here = (lax.axis_size(axis), lax.axis_index(axis))
    everything = jax.tree.map(lambda part: lax.all_gather(part, axis), array)
    start = jax.tree.map(
        lambda part, zero: jnp.broadcast_to(jnp.asarray(zero, part.dtype), part.shape),
        array,
        identity,
    )

    def step(k, before):
        reached = k < here
        new = combine(before, jax.tree.map(lambda part: part[k], everything))
        return jax.tree.map(lambda a, b: jnp.where(reached, a, b), new, before)

    return lax.fori_loop(0, length, step, start)


def entering(array, axis, join, neutral):
    count = lax.axis_size(axis)
    place = lax.axis_index(axis)
    ahead = count - 1 - place
    gathered = jax.tree.map(
        lambda a, kind: lax.all_gather(a.astype(kind), axis),
        array,
        jax.tree.map(lambda a: jnp.bfloat16 if a.dtype == jnp.float32 else a.dtype, array),
    )
    state = jax.tree.map(lambda a, e: jnp.zeros_like(a) + jnp.asarray(e, a.dtype), array, neutral)

    def one(step, state):
        source = count - 1 - step
        return join(
            state,
            jax.tree.map(
                lambda a, own: lax.dynamic_index_in_dim(a, source, 0, False).astype(own.dtype),
                gathered,
                array,
            ),
        )

    return lax.fori_loop(0, ahead, one, state)


def norm_gain(values, gain):
    return values * lax.rsqrt(jnp.mean(values * values, -1, keepdims=True) + norm_epsilon) * gain


def segment_ids(positions, lengths):
    seq_ends = jnp.cumsum(lengths, axis=-1)
    return jnp.sum((seq_ends[:, None, :] <= positions[None, :, None]).astype(jnp.int32), -1)


def combine(earlier, later):
    first_map = jnp.einsum("bhij,bhjk->bhik", earlier[0], later[0], precision=highest_precision)
    offset_map = (
        jnp.einsum("bhij,bhjk->bhik", earlier[1], later[0], precision=highest_precision) + later[1]
    )
    return (first_map, offset_map)


def block_recurrence(queries, key_rows, values, log_decay, beta_gate, resets):
    streams, seg_len, head_count, key_dim = queries.shape
    val_dim = values.shape[-1]
    block_count = seg_len // BLOCK

    def arrange(tensor):
        shaped = tensor.reshape((streams, block_count, BLOCK) + tensor.shape[2:])
        axis_order = (1, 0, 3, 2, 4) if tensor.ndim == 4 else (1, 0, 3, 2)
        return shaped.transpose(axis_order)

    reset_count = jnp.cumsum(resets.reshape(streams, block_count, BLOCK).transpose(1, 0, 2), -1)[
        :, :, None, :
    ]
    index_rows = jnp.arange(BLOCK)[:, None]
    index_cols = jnp.arange(BLOCK)[None, :]
    lower_incl = index_rows >= index_cols
    lower_strict = index_rows > index_cols

    def block_step(memory, inputs):
        q_block, k_block, v_block, d_block, b_block, z_block = inputs
        summed = jnp.cumsum(d_block, -1)
        inside = (z_block[..., :, None] == z_block[..., None, :]) & lower_incl
        decay_ratio = jnp.where(
            inside,
            jnp.exp(jnp.where(inside, summed[..., :, None] - summed[..., None, :], 0.0)),
            0.0,
        )
        from_start = jnp.where(z_block == 0, jnp.exp(summed), 0.0)
        key_gram = jnp.einsum("bhtd,bhsd->bhts", k_block, k_block, precision=highest_precision)
        coupling = jnp.where(lower_strict, b_block[..., :, None] * decay_ratio * key_gram, 0.0)
        carried = jnp.einsum("bhcd,bhmd->bhcm", k_block, memory, precision=highest_precision)
        source = (
            jnp.concatenate(
                [b_block[..., None] * v_block, jnp.zeros(k_block.shape, jnp.float32)], -1
            )
            - (b_block * from_start)[..., None] * carried
        )
        update = lax.linalg.triangular_solve(
            coupling, source, left_side=True, lower=True, unit_diagonal=True
        )
        scores = jnp.where(
            inside,
            decay_ratio
            * jnp.einsum("bhtd,bhsd->bhts", q_block, k_block, precision=highest_precision),
            0.0,
        )
        outputs = from_start[..., None] * jnp.einsum(
            "bhcd,bhmd->bhcm", q_block, memory, precision=highest_precision
        ) + jnp.einsum("bhts,bhsm->bhtm", scores, update, precision=highest_precision)
        weighted = update * decay_ratio[..., BLOCK - 1, :, None]
        memory = from_start[..., BLOCK - 1, None, None] * memory + jnp.einsum(
            "bhsm,bhsd->bhmd", weighted, k_block, precision=highest_precision
        )
        return (memory, outputs)

    start_memory = jnp.concatenate(
        [
            jnp.zeros((streams, head_count, val_dim, key_dim), jnp.float32),
            jnp.broadcast_to(
                jnp.eye(key_dim, dtype=jnp.float32), (streams, head_count, key_dim, key_dim)
            ),
        ],
        2,
    )
    last_memory, outputs = lax.scan(
        block_step,
        start_memory,
        (
            arrange(queries),
            arrange(key_rows),
            arrange(values),
            arrange(log_decay),
            arrange(beta_gate),
            reset_count,
        ),
    )
    outputs = outputs.transpose(1, 0, 3, 2, 4).reshape(
        streams, seg_len, head_count, val_dim + key_dim
    )
    return (outputs, last_memory)


def finish(span_out, state_in, gate_raw, gain_out):
    streams, seg_len, head_count = (span_out.shape[0], span_out.shape[1], span_out.shape[2])
    val_dim = state_in.shape[2]
    direct = span_out[..., :val_dim] + jnp.einsum(
        "bhvd,bshd->bshv", state_in, span_out[..., val_dim:], precision=highest_precision
    )
    scaled = (
        direct * lax.rsqrt(jnp.mean(direct * direct, -1, keepdims=True) + norm_epsilon) * gain_out
    )
    gated_output = scaled * jax.nn.silu(gate_raw.reshape(streams, seg_len, head_count, val_dim))
    return gated_output.reshape(streams, seg_len, head_count * val_dim)


def on_device(
    tokens,
    lengths,
    w_q,
    w_k,
    w_v,
    w_g,
    w_a,
    w_b,
    output_weight,
    w_gate,
    w_up,
    w_down,
    gain_attn,
    gain_ffn,
    gain_out,
    conv_q,
    conv_k,
    conv_v,
    a_log,
    dt_bias,
    d_out,
):
    gathered = (
        lax.all_gather(w_q, ("dp", "ctx"), axis=0, tiled=True),
        lax.all_gather(w_k, ("dp", "ctx"), axis=0, tiled=True),
        lax.all_gather(w_v, ("dp", "ctx"), axis=0, tiled=True),
        lax.all_gather(w_g, ("dp", "ctx"), axis=0, tiled=True),
        lax.all_gather(w_a, ("dp", "ctx"), axis=0, tiled=True),
        lax.all_gather(w_b, ("dp", "ctx"), axis=0, tiled=True),
        lax.all_gather(output_weight, ("dp", "ctx"), axis=0, tiled=True),
        lax.all_gather(w_gate, ("dp", "ctx"), axis=0, tiled=True),
        lax.all_gather(w_up, ("dp", "ctx"), axis=0, tiled=True),
        lax.all_gather(w_down, ("dp", "ctx"), axis=0, tiled=True),
        lax.all_gather(gain_attn, ("dp", "ctx"), axis=0, tiled=True),
        lax.all_gather(gain_ffn, ("dp", "ctx"), axis=0, tiled=True),
        lax.all_gather(gain_out, ("dp", "ctx"), axis=0, tiled=True),
    )
    streams, seg_len = (tokens.shape[0], tokens.shape[1])
    head_count = a_log.shape[0]
    key_cols = gathered[0].shape[1]
    val_cols = gathered[2].shape[1]
    key_dim = key_cols // head_count
    val_dim = val_cols // head_count
    hidden_cols = gathered[7].shape[1]
    conv_width = conv_q.shape[0]
    mixed_cols = 2 * key_cols + val_cols
    halo_rows = conv_width - 1
    positions = (
        lax.axis_index("ctx") * seg_len
        - halo_rows
        + jnp.arange(seg_len + halo_rows, dtype=jnp.int32)
    )
    segment = segment_ids(positions, lengths)
    own_segment = segment[:, halo_rows:]
    tap_masks = [
        (
            (segment[:, offset : offset + seg_len] == own_segment)
            & (positions[offset : offset + seg_len] >= 0)[None, :]
        ).astype(jnp.float32)[..., None]
        for offset in range(conv_width)
    ]
    keep_mask = (own_segment == segment[:, halo_rows - 1 : halo_rows - 1 + seg_len]) & (
        positions[halo_rows:] > 0
    )[None, :]
    resets = 1 - keep_mask.astype(jnp.int32)
    tokens_f = tokens.astype(jnp.float32)
    gain_attn_f = gathered[10].astype(jnp.float32)
    gain_ffn_f = gathered[11].astype(jnp.float32)
    normed = norm_gain(tokens_f, gain_attn_f).astype(jnp.bfloat16)
    w_main = jnp.concatenate([gathered[0], gathered[1], gathered[2], gathered[3]], 1)
    w_side = jnp.concatenate([gathered[4], gathered[5]], 1)
    projected = jnp.einsum("bsd,dc->bsc", normed, w_main, preferred_element_type=jnp.float32)
    mixed_raw = projected[..., :mixed_cols].astype(jnp.bfloat16)
    gate_raw = projected[..., mixed_cols:]
    side_raw = jnp.einsum("bsd,dc->bsc", normed, w_side, preferred_element_type=jnp.float32)
    halo = from_behind(mixed_raw[:, seg_len - halo_rows :], "ctx", 1)
    raw_ext = jnp.concatenate([halo, mixed_raw], 1).astype(jnp.float32)
    conv_all = jnp.concatenate([conv_q, conv_k, conv_v], 1).astype(jnp.float32)

    def prepare(raw_cols, side_cols, conv_weight, log_rate, rate_bias):
        summed = raw_cols[:, 0:seg_len] * conv_weight[0] * tap_masks[0]
        for offset in range(1, conv_width):
            summed = (
                summed
                + raw_cols[:, offset : offset + seg_len] * conv_weight[offset] * tap_masks[offset]
            )
        active = jax.nn.silu(summed)
        queries = active[..., :key_cols].reshape(streams, seg_len, head_count, key_dim)
        key_rows = active[..., key_cols : 2 * key_cols].reshape(
            streams, seg_len, head_count, key_dim
        )
        values = active[..., 2 * key_cols :].reshape(streams, seg_len, head_count, val_dim)
        queries = (
            queries
            * lax.rsqrt(jnp.sum(queries * queries, -1, keepdims=True) + unit_epsilon)
            * key_dim ** (-0.5)
        )
        key_rows = key_rows * lax.rsqrt(
            jnp.sum(key_rows * key_rows, -1, keepdims=True) + unit_epsilon
        )
        log_decay = -jnp.exp(log_rate) * jax.nn.softplus(side_cols[..., :head_count] + rate_bias)
        beta_gate = jax.nn.sigmoid(side_cols[..., head_count:])
        return (queries, key_rows, values, log_decay, beta_gate)

    prepared, pull_prepare = jax.vjp(prepare, raw_ext, side_raw, conv_all, a_log, dt_bias)
    span_result, pull_span = jax.vjp(
        partial(block_recurrence, resets=resets),
        prepared[0],
        prepared[1],
        prepared[2],
        prepared[3],
        prepared[4],
    )
    span_out, last_memory = span_result
    transit = last_memory[:, :, val_dim:, :]
    local_state = last_memory[:, :, :val_dim, :]
    eye_state = jnp.broadcast_to(jnp.eye(key_dim, dtype=jnp.float32), transit.shape)
    zero_state = jnp.zeros(local_state.shape, jnp.float32)
    state_in = prefix((transit, local_state), "ctx", combine, (eye_state, zero_state))[1]
    gated_f, pull_finish = jax.vjp(
        finish, span_out, state_in, gate_raw, gathered[12].astype(jnp.float32)
    )
    gated = gated_f.astype(jnp.bfloat16)
    attn_part = jnp.einsum("bsc,dc->bsd", gated, gathered[6], preferred_element_type=jnp.float32)
    middle = tokens_f + lax.psum(attn_part, "tp")
    normed_full, pull_second = jax.vjp(norm_gain, middle, gain_ffn_f)
    normed_ffn = normed_full.astype(jnp.bfloat16)
    w_pair = jnp.concatenate([gathered[7], gathered[8]], 1)
    paired = jnp.einsum("bsd,dc->bsc", normed_ffn, w_pair, preferred_element_type=jnp.float32)
    gate_val = paired[..., :hidden_cols]
    up_val = paired[..., hidden_cols:]
    hidden = (jax.nn.silu(gate_val) * up_val).astype(jnp.bfloat16)
    ffn_part = jnp.einsum("bsf,df->bsd", hidden, gathered[9], preferred_element_type=jnp.float32)
    layer_out = (middle + lax.psum(ffn_part.astype(jnp.bfloat16), "tp").astype(jnp.float32)).astype(
        jnp.bfloat16
    )
    cotangent = d_out.astype(jnp.float32)
    d_hidden = jnp.einsum("bsd,df->bsf", d_out, gathered[9], preferred_element_type=jnp.float32)
    grad_down = jnp.einsum("bsd,bsf->df", d_out, hidden, preferred_element_type=jnp.float32)
    sig_gate = jax.nn.sigmoid(gate_val)
    d_gate = (d_hidden * up_val * sig_gate * (1.0 + gate_val * (1.0 - sig_gate))).astype(
        jnp.bfloat16
    )
    d_up = (d_hidden * gate_val * sig_gate).astype(jnp.bfloat16)
    d_paired = jnp.concatenate([d_gate, d_up], -1)
    grad_pair = jnp.einsum("bsd,bsc->dc", normed_ffn, d_paired, preferred_element_type=jnp.float32)
    d_ffn_part = jnp.einsum("bsc,dc->bsd", d_paired, w_pair, preferred_element_type=jnp.float32)
    d_middle_norm, grad_gain_ffn = pull_second(lax.psum(d_ffn_part, "tp"))
    d_middle = cotangent + d_middle_norm
    d_attention = d_middle.astype(jnp.bfloat16)
    grad_out_proj = jnp.einsum(
        "bsd,bsc->dc", d_attention, gated, preferred_element_type=jnp.float32
    )
    d_gated = jnp.einsum(
        "bsd,dc->bsc", d_attention, gathered[6], preferred_element_type=jnp.float32
    )
    d_span, d_state_in, d_gate_raw, grad_gain_out = pull_finish(d_gated)
    d_state_out = entering(
        (jnp.swapaxes(transit, -1, -2), d_state_in), "ctx", combine, (eye_state, zero_state)
    )[1]
    d_transit = jnp.einsum("bhvd,bhve->bhde", state_in, d_state_out, precision=highest_precision)
    d_prepared = pull_span((d_span, jnp.concatenate([d_state_out, d_transit], 2)))
    d_raw_ext, d_side, d_conv, d_log_rate, d_rate_bias = pull_prepare(d_prepared)
    returned = from_behind(d_raw_ext[:, :halo_rows], "ctx", -1)
    d_raw = d_raw_ext[:, halo_rows:]
    d_raw = jnp.concatenate(
        [d_raw[:, : seg_len - halo_rows], d_raw[:, seg_len - halo_rows :] + returned], 1
    )
    d_projected = jnp.concatenate([d_raw, d_gate_raw], -1).astype(jnp.bfloat16)
    d_side_low = d_side.astype(jnp.bfloat16)
    grad_main = jnp.einsum("bsd,bsc->dc", normed, d_projected, preferred_element_type=jnp.float32)
    grad_side = jnp.einsum("bsd,bsc->dc", normed, d_side_low, preferred_element_type=jnp.float32)
    d_normed_part = jnp.einsum(
        "bsc,dc->bsd", d_projected, w_main, preferred_element_type=jnp.float32
    ) + jnp.einsum("bsc,dc->bsd", d_side_low, w_side, preferred_element_type=jnp.float32)
    d_normed, grad_gain_out = (
        lax.psum(d_normed_part.astype(jnp.bfloat16), "tp").astype(jnp.float32),
        lax.psum(grad_gain_out.astype(jnp.bfloat16), "tp").astype(jnp.float32),
    )
    recomputed, pull_first = jax.vjp(norm_gain, tokens_f, gain_attn_f)
    d_tokens_norm, grad_gain_attn = pull_first(d_normed)
    grad_tokens = d_middle + d_tokens_norm
    grads = (
        lax.psum_scatter(grad_main[:, :key_cols], ("dp", "ctx"), scatter_dimension=0, tiled=True),
        lax.psum_scatter(
            grad_main[:, key_cols : 2 * key_cols], ("dp", "ctx"), scatter_dimension=0, tiled=True
        ),
        lax.psum_scatter(
            grad_main[:, 2 * key_cols : mixed_cols], ("dp", "ctx"), scatter_dimension=0, tiled=True
        ),
        lax.psum_scatter(grad_main[:, mixed_cols:], ("dp", "ctx"), scatter_dimension=0, tiled=True),
        lax.psum_scatter(grad_side[:, :head_count], ("dp", "ctx"), scatter_dimension=0, tiled=True),
        lax.psum_scatter(grad_side[:, head_count:], ("dp", "ctx"), scatter_dimension=0, tiled=True),
        lax.psum_scatter(grad_out_proj, ("dp", "ctx"), scatter_dimension=0, tiled=True),
        lax.psum_scatter(
            grad_pair[:, :hidden_cols], ("dp", "ctx"), scatter_dimension=0, tiled=True
        ),
        lax.psum_scatter(
            grad_pair[:, hidden_cols:], ("dp", "ctx"), scatter_dimension=0, tiled=True
        ),
        lax.psum_scatter(grad_down, ("dp", "ctx"), scatter_dimension=0, tiled=True),
        lax.psum_scatter(grad_gain_attn, ("dp", "ctx"), scatter_dimension=0, tiled=True),
        lax.psum_scatter(grad_gain_ffn, ("dp", "ctx"), scatter_dimension=0, tiled=True),
        lax.psum_scatter(grad_gain_out, ("dp", "ctx"), scatter_dimension=0, tiled=True),
    )
    smalls = lax.psum(
        (
            d_conv[:, :key_cols],
            d_conv[:, key_cols : 2 * key_cols],
            d_conv[:, 2 * key_cols :],
            d_log_rate,
            d_rate_bias,
        ),
        ("dp", "ctx"),
    )
    return (
        layer_out,
        grad_tokens,
        grads[0],
        grads[1],
        grads[2],
        grads[3],
        grads[4],
        grads[5],
        grads[6],
        grads[7],
        grads[8],
        grads[9],
        grads[10],
        grads[11],
        grads[12],
        smalls[0],
        smalls[1],
        smalls[2],
        smalls[3],
        smalls[4],
    )


def solution(mesh):
    return jax.shard_map(
        on_device,
        mesh=mesh,
        in_specs=(
            P("dp", "ctx", None),
            P("dp", None),
            P(("dp", "ctx"), "tp"),
            P(("dp", "ctx"), "tp"),
            P(("dp", "ctx"), "tp"),
            P(("dp", "ctx"), "tp"),
            P(("dp", "ctx"), "tp"),
            P(("dp", "ctx"), "tp"),
            P(("dp", "ctx"), "tp"),
            P(("dp", "ctx"), "tp"),
            P(("dp", "ctx"), "tp"),
            P(("dp", "ctx"), "tp"),
            P(("dp", "ctx")),
            P(("dp", "ctx")),
            P(("dp", "ctx")),
            P(None, "tp"),
            P(None, "tp"),
            P(None, "tp"),
            P("tp"),
            P("tp"),
            P("dp", "ctx", None),
        ),
        out_specs=(
            P("dp", "ctx", None),
            P("dp", "ctx", None),
            P(("dp", "ctx"), "tp"),
            P(("dp", "ctx"), "tp"),
            P(("dp", "ctx"), "tp"),
            P(("dp", "ctx"), "tp"),
            P(("dp", "ctx"), "tp"),
            P(("dp", "ctx"), "tp"),
            P(("dp", "ctx"), "tp"),
            P(("dp", "ctx"), "tp"),
            P(("dp", "ctx"), "tp"),
            P(("dp", "ctx"), "tp"),
            P(("dp", "ctx")),
            P(("dp", "ctx")),
            P(("dp", "ctx")),
            P(None, "tp"),
            P(None, "tp"),
            P(None, "tp"),
            P("tp"),
            P("tp"),
        ),
        check_vma=False,
    )
```

profile of v0, /device:TPU:0, one launch (start us, length us, event | category | flops | bytes accessed | tf_op | source)
XLA Modules:
  0.0 3245.3 jit_solution(3402025657115890803)
XLA Ops:
  13.3 22.2 all-gather.4
  72.5 32.5 %all_gather.66 = bf16[1024,256]{1,0:T(8,128)(2,1)S(1)} all-gather(bf16[128,256]{1,0:T(8,128)(2,1)S(1)} %copy-done.55), channel_id=1, replica_groups=mesh['dp'=4,'ctx'=2,'tp'=4] {'dp','ctx'}, dimensions={0}, use_global_device_ids=true | all-gather | bytes 589824 | tf_op jit(solution)/shard_map/all_gather | solution.py:200
  105.0 31.2 all_gather.67
  214.0 629.3 %while.118 = (s32[]{:T(128)}, f32[2,2,384,128]{3,2,1,0:T(8,128)S(1)}, f32[16,2,2,64,384]{4,3,2,1,0:T(8,128)}, pred[16,2,2,64,64]{4,3,2,1,0:T(32,128)(4,1)}, f32[...) while((s32[]{:T(128)}, ...), condition=%wide.region_8.9_spmd.clone, body=%wide.region_6.8_spmd.clone.sunk | while | flops 655819968 | bytes 12884393 | solution.py:145
  216.5 19.7 custom-call.46
  255.7 19.7 custom-call.46
  295.1 19.7 custom-call.46
  334.4 19.7 custom-call.46
  373.7 19.7 custom-call.46
  413.1 19.7 custom-call.46
  452.4 19.7 custom-call.46
  491.7 19.7 custom-call.46
  531.0 19.7 custom-call.46
  570.3 19.7 custom-call.46
  609.6 19.7 custom-call.46
  648.8 19.7 custom-call.46
  688.2 19.7 custom-call.46
  727.5 19.7 custom-call.46
  766.8 19.7 custom-call.46
  806.2 19.7 custom-call.46
  935.6 130.1 %all-reduce.29.cloned.1.call-done = f32[2,1024,1024]{2,1,0:T(8,128)} async-done(((f32[2,1024,1024]{2,1,0:T(8,128)}), f32[2,1024,1024]{2,1,0:T(8,128)}) %all-reduce.29.cloned.1.call-update) | async-done | bytes 8388624 | tf_op jit(solution)/shard_map/psum | solution.py:301
  1074.7 38.0 %all-gather.20.cloned.1.call-done = bf16[1024,704]{1,0:T(8,128)(2,1)} async-done(((bf16[128,704]{1,0:T(8,128)(2,1)}), bf16[1024,704]{1,0:T(8,128)(2,1)}) %all-gather.20.cloned.1.call-update) | async-done | bytes 1441808 | tf_op jit(solution)/shard_map/all_gather | solution.py:207
  1112.7 45.8 %all-gather.22.cloned.1.call-done = bf16[1024,704]{1,0:T(8,128)(2,1)} async-done(((bf16[128,704]{1,0:T(8,128)(2,1)}), bf16[1024,704]{1,0:T(8,128)(2,1)}) %all-gather.22.cloned.1.call-update) | async-done | bytes 1441808 | tf_op jit(solution)/shard_map/all_gather | solution.py:208
  1172.1 31.0 all-gather.24.cloned.1.call-done
  1232.3 145.4 %all-reduce.31.cloned.1.call-done = f32[2,1024,1024]{2,1,0:T(8,128)} async-done(((f32[2,1024,1024]{2,1,0:T(8,128)}), f32[2,1024,1024]{2,1,0:T(8,128)}) %all-reduce.31.cloned.1.call-update) | async-done | bytes 8388624 | tf_op jit(solution)/shard_map/psum | solution.py:324
  1449.0 925.4 %while.119 = (s32[]{:T(128)}, f32[2,2,384,128]{3,2,1,0:T(8,128)S(1)}, f32[16,2,2,64,128]{4,3,2,1,0:T(8,128)}, f32[16,2,2,64,128]{4,3,2,1,0:T(8,128)}, f32[16,2,2...) while((s32[]{:T(128)}, ...), condition=%wide.region_30.31_spmd.clone, body=%wide.region_20.30_spmd.clone.sunk | while | flops 1324413696 | bytes 21210372 | solution.py:145
  1457.9 19.7 custom-call.47
  1515.7 19.7 custom-call.47
  1573.5 19.7 custom-call.47
  1631.4 19.7 custom-call.47
  1689.2 19.7 custom-call.47
  1747.0 19.7 custom-call.47
  1804.8 19.7 custom-call.47
  1862.6 19.7 custom-call.47
  1920.4 19.7 custom-call.47
  1978.2 19.7 custom-call.47
  2035.9 19.7 custom-call.47
  2151.6 19.7 custom-call.47
  2209.4 19.7 custom-call.47
  2325.0 19.7 custom-call.47
  2604.3 56.0 %reduce-scatter.27.cloned.1.call-done = f32[128,704]{1,0:T(8,128)} async-done(((f32[1024,704]{1,0:T(8,128)}), f32[128,704]{1,0:T(8,128)}) %reduce-scatter.27.cloned.1.call-update) | async-done | bytes 360464 | tf_op jit(solution)/shard_map/reduce_scatter | solution.py:374
  2662.2 153.5 %all-reduce.33.cloned.1.call-done = (bf16[2,1024,1024]{2,1,0:T(8,128)(2,1)}, bf16[2,1024,1024]{2,1,0:T(8,128)(2,1)}) async-done(((bf16[2,1024,1024]{2,1,0:T(8,128)(2,1)}, bf16[2,1024,1024]{2,1,0:T(8,128)(2,1)}), (bf16[2,1024,1024]{2,1,0:T(8,128)(2,1)}, bf16[2,1024,1024]{2,1,0:T(8,128)(2,1)})) %all-reduce.33.cloned.1.call-update) | async-done | bytes 8388624 | tf_op jit(solution)/shard_map/psum | solution.py:310
  2821.9 38.4 %all-reduce.23 = (f32[1024]{0:T(1024)S(1)}, f32[1024]{0:T(1024)S(1)}, f32[256]{0:T(256)S(1)}, f32[4,256]{1,0:T(4,128)}, f32[4,256]{1,0:T(4,128)}, /*index=5*/f32[4,512]{1,0:T(4,128)}, f32[2]{0:T(128)}, f32[2]{0:T(128)}) all-reduce(f32[1024]{0:T(1024)S(1)} %get-tuple-element.2345, ...), channel_id=16, replica_groups=mesh['dp'=4,'ctx'=2,'tp'=4] {'dp','ctx'}, use_global_device_ids=true, to_apply=%region_46.47.clone | all-reduce | flops 6404 | bytes 50720
  2892.4 66.5 %reduce-scatter.15.cloned.1.call-done = f32[128,256]{1,0:T(8,128)} async-done(((f32[1024,256]{1,0:T(8,128)}), f32[128,256]{1,0:T(8,128)}) %reduce-scatter.15.cloned.1.call-update) | async-done | bytes 131088 | tf_op jit(solution)/shard_map/reduce_scatter | solution.py:360
  2958.9 66.6 %reduce-scatter.17.cloned.1.call-done = f32[128,256]{1,0:T(8,128)} async-done(((f32[1024,256]{1,0:T(8,128)}), f32[128,256]{1,0:T(8,128)}) %reduce-scatter.17.cloned.1.call-update) | async-done | bytes 131088 | tf_op jit(solution)/shard_map/reduce_scatter | solution.py:361
  3025.5 70.9 %reduce-scatter.23.cloned.1.call-done = f32[128,512]{1,0:T(8,128)} async-done(((f32[1024,512]{1,0:T(8,128)}), f32[128,512]{1,0:T(8,128)}) %reduce-scatter.23.cloned.1.call-update) | async-done | bytes 262160 | tf_op jit(solution)/shard_map/reduce_scatter | solution.py:370
  3096.4 71.0 %reduce-scatter.19.cloned.1.call-done = f32[128,512]{1,0:T(8,128)} async-done(((f32[1024,512]{1,0:T(8,128)}), f32[128,512]{1,0:T(8,128)}) %reduce-scatter.19.cloned.1.call-update) | async-done | bytes 262160 | tf_op jit(solution)/shard_map/reduce_scatter | solution.py:364
  3167.4 70.8 %reduce-scatter.21.cloned.1.call-done = f32[128,512]{1,0:T(8,128)} async-done(((f32[1024,512]{1,0:T(8,128)}), f32[128,512]{1,0:T(8,128)}) %reduce-scatter.21.cloned.1.call-update) | async-done | bytes 262160 | tf_op jit(solution)/shard_map/reduce_scatter | solution.py:367
  (1473 shorter events, 1568.0 us)
Async XLA Ops:
  7.3 129.0 %all-gather.14.cloned.1.call-start = ((), (), s32[]{:S(2)}) async-start(), calls=%async_computation.10 | async-start | bytes 1179648 | tf_op jit(solution)/shard_map/all_gather | solution.py:202
  8.0 128.2 %all-gather.16.cloned.1.call-start = ((), (), s32[]{:S(2)}) async-start(), calls=%async_computation.11 | async-start | bytes 1179648 | tf_op jit(solution)/shard_map/all_gather | solution.py:203
  8.7 872.0 %all-gather.26.cloned.1.call-start = ((), (), s32[]{:S(2)}) async-start(), calls=%async_computation.26 | async-start | bytes 1572864 | tf_op jit(solution)/shard_map/all_gather | solution.py:24
  8.9 149.9 %copy-start.58 = (f32[1024]{0:T(1024)}, f32[1024]{0:T(1024)S(1)}, u32[]{:S(2)}) copy-start(f32[1024]{0:T(1024)S(1)} %get-tuple-element.2594) | copy-start | bytes 12292
  9.8 60.7 %copy-start.3 = (bf16[2,1024,1024]{2,1,0:T(8,128)(2,1)S(1)}, bf16[2,1024,1024]{2,1,0:T(8,128)(2,1)}, u32[]{:S(2)}) copy-start(bf16[2,1024,1024]{2,1,0:T(8,128)(2,1)} %param.29) | copy-start | bytes 12582916
  13.1 57.1 %copy-start.51 = (f32[2,1024]{1,0:T(2,128)}, f32[2,1024]{1,0:T(2,128)S(1)}, u32[]{:S(2)}) copy-start(f32[2,1024]{1,0:T(2,128)S(1)} %fusion.172) | copy-start | bytes 24580
  13.1 58.7 %copy-start.82 = (f32[2]{0:T(128)S(1)}, f32[2]{0:T(128)}, u32[]{:S(2)}) copy-start(f32[2]{0:T(128)} %param.48) | copy-start | bytes 28
  13.1 59.4 %copy-start.55 = (bf16[128,256]{1,0:T(8,128)(2,1)S(1)}, bf16[128,256]{1,0:T(8,128)(2,1)}, u32[]{:S(2)}) copy-start(bf16[128,256]{1,0:T(8,128)(2,1)} %param.31) | copy-start | bytes 196612
  13.2 123.0 %copy-start.49 = (f32[2,1024]{1,0:T(2,128)}, f32[2,1024]{1,0:T(2,128)S(1)}, u32[]{:S(2)}) copy-start(f32[2,1024]{1,0:T(2,128)S(1)} %fusion.238) | copy-start | bytes 24580
  13.2 58.5 %copy-start.84 = (f32[2]{0:T(128)}, f32[2]{0:T(128)S(1)}, u32[]{:S(2)}) copy-start(f32[2]{0:T(128)S(1)} %exponential_negate_fusion) | copy-start | bytes 28
  35.4 100.8 %copy-start.60 = (f32[8,1,128]{2,1,0:T(1,128)}, f32[8,1,128]{2,1,0:T(1,128)S(1)}, u32[]{:S(2)}) copy-start(f32[8,1,128]{2,1,0:T(1,128)S(1)} %convert_element_type.150) | copy-start | bytes 12292
  51.6 53.4 %copy-start.72 = (bf16[1024,2]{0,1:T(2,128)(2,1)}, bf16[1024,2]{0,1:T(2,128)(2,1)S(1)}, u32[]{:S(2)}) copy-start(bf16[1024,2]{0,1:T(2,128)(2,1)S(1)} %all_gather.64) | copy-start | bytes 12292
  70.0 88.8 %copy-start.62 = (f32[1,1024]{1,0:T(1,128)}, f32[1,1024]{1,0:T(1,128)S(1)}, u32[]{:S(2)}) copy-start(f32[1,1024]{1,0:T(1,128)S(1)} %get-tuple-element.2586) | copy-start | bytes 12292
  70.0 88.8 %copy-start.64 = (f32[1,1024]{1,0:T(1,128)}, f32[1,1024]{1,0:T(1,128)S(1)}, u32[]{:S(2)}) copy-start(f32[1,1024]{1,0:T(1,128)S(1)} %get-tuple-element.2587) | copy-start | bytes 12292
  70.0 88.8 %copy-start.66 = (f32[1,1024]{1,0:T(1,128)}, f32[1,1024]{1,0:T(1,128)S(1)}, u32[]{:S(2)}) copy-start(f32[1,1024]{1,0:T(1,128)S(1)} %get-tuple-element.2588) | copy-start | bytes 12292
  70.1 88.8 %copy-start.68 = (f32[1,1024]{1,0:T(1,128)}, f32[1,1024]{1,0:T(1,128)S(1)}, u32[]{:S(2)}) copy-start(f32[1,1024]{1,0:T(1,128)S(1)} %get-tuple-element.2589) | copy-start | bytes 12292
  70.2 88.7 %copy-start.43 = (f32[2,1024]{1,0:T(2,128)}, f32[2,1024]{1,0:T(2,128)S(1)}, u32[]{:S(2)}) copy-start(f32[2,1024]{1,0:T(2,128)S(1)} %get-tuple-element.2590) | copy-start | bytes 24580
  70.2 88.7 %copy-start.45 = (f32[2,1024]{1,0:T(2,128)}, f32[2,1024]{1,0:T(2,128)S(1)}, u32[]{:S(2)}) copy-start(f32[2,1024]{1,0:T(2,128)S(1)} %get-tuple-element.2591) | copy-start | bytes 24580
  70.2 88.7 %copy-start.47 = (f32[2,1024]{1,0:T(2,128)}, f32[2,1024]{1,0:T(2,128)S(1)}, u32[]{:S(2)}) copy-start(f32[2,1024]{1,0:T(2,128)S(1)} %get-tuple-element.2592) | copy-start | bytes 24580
  71.8 78.0 %copy-start.53 = (f32[2,1024,4]{1,2,0:T(4,128)}, f32[2,1024,4]{1,2,0:T(4,128)S(1)}, u32[]{:S(2)}) copy-start(f32[2,1024,4]{1,2,0:T(4,128)S(1)} %fusion.218) | copy-start | bytes 98308
  72.5 82.2 %copy-start.41 = (f32[2,1024,2]{1,2,0:T(2,128)}, f32[2,1024,2]{1,2,0:T(2,128)S(1)}, u32[]{:S(2)}) copy-start(f32[2,1024,2]{1,2,0:T(2,128)S(1)} %get-tuple-element.2579) | copy-start | bytes 49156
  152.5 5.1 collective-permute-start
  214.0 630.9 %copy-start.81 = (u32[32]{0:T(128)S(1)}, u32[32]{0:T(128)}, u32[]{:S(2)}) copy-start(u32[32]{0:T(128)} %constant.376) | copy-start | bytes 388
  844.2 62.1 %all-gather.18.cloned.1.call-start = ((), (), s32[]{:S(2)}) async-start(), calls=%async_computation.12 | async-start | bytes 1179648 | tf_op jit(solution)/shard_map/all_gather | solution.py:206
  844.8 220.9 %all-reduce.29.cloned.1.call-start = ((), (), s32[]{:S(2)}) async-start(), calls=%async_computation.13 | async-start | bytes 16777216 | tf_op jit(solution)/shard_map/psum | solution.py:301
  913.9 198.7 %all-gather.20.cloned.1.call-start = ((), (), s32[]{:S(2)}) async-start(), calls=%async_computation.14 | async-start | bytes 1769472 | tf_op jit(solution)/shard_map/all_gather | solution.py:207
  915.7 242.8 %all-gather.22.cloned.1.call-start = ((), (), s32[]{:S(2)}) async-start(), calls=%async_computation.15 | async-start | bytes 1769472 | tf_op jit(solution)/shard_map/all_gather | solution.py:208
  916.6 286.6 %all-gather.24.cloned.1.call-start = ((), (), s32[]{:S(2)}) async-start(), calls=%async_computation.16 | async-start | bytes 1622016 | tf_op jit(solution)/shard_map/all_gather | solution.py:209
  917.3 460.4 %all-reduce.31.cloned.1.call-start = ((), (), s32[]{:S(2)}) async-start(), calls=%async_computation.17 | async-start | bytes 16777216 | tf_op jit(solution)/shard_map/psum | solution.py:324
  1226.3 1373.2 %reduce-scatter.31.cloned.1.call-start = ((), (), s32[]{:S(2)}) async-start(), calls=%async_computation.27 | async-start | bytes 589824
  1448.9 925.6 %copy-start.42 = (f32[2,1024,2]{1,2,0:T(2,128)S(1)}, f32[2,1024,2]{1,2,0:T(2,128)}, u32[]{:S(2)}) copy-start(f32[2,1024,2]{1,2,0:T(2,128)} %copy-done.41) | copy-start | bytes 49156
  1448.9 925.7 %copy-start.54 = (f32[2,1024,4]{1,2,0:T(4,128)S(1)}, f32[2,1024,4]{1,2,0:T(4,128)}, u32[]{:S(2)}) copy-start(f32[2,1024,4]{1,2,0:T(4,128)} %copy-done.53) | copy-start | bytes 98308
  1448.9 925.7 %copy-start.57 = (f32[2,1024,2]{1,2,0:T(2,128)S(1)}, f32[2,1024,2]{1,2,0:T(2,128)}, u32[]{:S(2)}) copy-start(f32[2,1024,2]{1,2,0:T(2,128)} %get-tuple-element.2520) | copy-start | bytes 49156
  1448.9 925.7 %copy-start.83 = (f32[2]{0:T(128)S(1)}, f32[2]{0:T(128)}, u32[]{:S(2)}) copy-start(f32[2]{0:T(128)} %param.48) | copy-start | bytes 28
  1448.9 925.7 %copy-start.85 = (f32[2]{0:T(128)S(1)}, f32[2]{0:T(128)}, u32[]{:S(2)}) copy-start(f32[2]{0:T(128)} %copy-done.84) | copy-start | bytes 28
  1448.9 926.5 %copy-start.50 = (f32[2,1024]{1,0:T(2,128)S(1)}, f32[2,1024]{1,0:T(2,128)}, u32[]{:S(2)}) copy-start(f32[2,1024]{1,0:T(2,128)} %copy-done.49) | copy-start | bytes 24580
  1448.9 926.4 %copy-start.61 = (f32[8,1,128]{2,1,0:T(1,128)S(1)}, f32[8,1,128]{2,1,0:T(1,128)}, u32[]{:S(2)}) copy-start(f32[8,1,128]{2,1,0:T(1,128)} %copy-done.60) | copy-start | bytes 12292
  2379.8 221.2 %reduce-scatter.33.cloned.1.call-start = ((), (), s32[]{:S(2)}) async-start(), calls=%async_computation.28 | async-start | bytes 589824
  2395.7 206.8 %reduce-scatter.25.cloned.1.call-start = ((), (), s32[]{:S(2)}) async-start(), calls=%async_computation.23 | async-start | bytes 3538944 | tf_op jit(solution)/shard_map/reduce_scatter | solution.py:371
  2402.1 258.2 %reduce-scatter.27.cloned.1.call-start = ((), (), s32[]{:S(2)}) async-start(), calls=%async_computation.24 | async-start | bytes 3538944 | tf_op jit(solution)/shard_map/reduce_scatter | solution.py:374
  2410.6 405.1 %all-reduce.33.cloned.1.call-start = ((), (), s32[]{:S(2)}) async-start(), calls=%async_computation.29 | async-start | bytes 16777216 | tf_op jit(solution)/shard_map/psum | solution.py:310
  2516.6 24.4 collective-permute-start.1
  2555.1 337.4 %reduce-scatter.29.cloned.1.call-start = ((), (), s32[]{:S(2)}) async-start(), calls=%async_computation.25 | async-start | bytes 3244032 | tf_op jit(solution)/shard_map/reduce_scatter | solution.py:377
  2563.0 395.9 %reduce-scatter.15.cloned.1.call-start = ((), (), s32[]{:S(2)}) async-start(), calls=%async_computation.18 | async-start | bytes 1179648 | tf_op jit(solution)/shard_map/reduce_scatter | solution.py:360
  2578.4 447.1 %reduce-scatter.17.cloned.1.call-start = ((), (), s32[]{:S(2)}) async-start(), calls=%async_computation.19 | async-start | bytes 1179648 | tf_op jit(solution)/shard_map/reduce_scatter | solution.py:361
  2579.0 517.4 %reduce-scatter.23.cloned.1.call-start = ((), (), s32[]{:S(2)}) async-start(), calls=%async_computation.22 | async-start | bytes 2359296 | tf_op jit(solution)/shard_map/reduce_scatter | solution.py:370
  2586.4 581.0 %reduce-scatter.19.cloned.1.call-start = ((), (), s32[]{:S(2)}) async-start(), calls=%async_computation.20 | async-start | bytes 2359296 | tf_op jit(solution)/shard_map/reduce_scatter | solution.py:364
  2591.2 647.0 %reduce-scatter.21.cloned.1.call-start = ((), (), s32[]{:S(2)}) async-start(), calls=%async_computation.21 | async-start | bytes 2359296 | tf_op jit(solution)/shard_map/reduce_scatter | solution.py:367
  (108 other events, 899.9 us)
Sparse Core Ops, SparseCore 0:
  10.2 42.9 all-gather.13
  55.3 41.2 all-gather.15
  844.3 20.6 all-gather.25
  867.0 39.2 all-gather.17
  914.0 151.5 all-reduce.28
  1068.3 44.3 all-gather.19
  1115.4 42.9 all-gather.21
  1160.5 42.6 all-gather.23
  1226.4 151.2 all-reduce.30
  2379.9 61.5 reduce-scatter.30
  2445.3 60.9 reduce-scatter.32
  2509.7 73.3 reduce-scatter.24
  2586.7 73.5 reduce-scatter.26
  2663.3 152.3 all-reduce.32
  2819.7 72.7 reduce-scatter.28
  2896.3 62.5 reduce-scatter.14
  2963.1 62.2 reduce-scatter.16
  3029.4 66.9 reduce-scatter.22
  3100.5 66.8 reduce-scatter.18
  3171.3 66.8 reduce-scatter.20
where the time goes:
time: 3260 us; the launch traced here: 3250 us
  waiting for transfers between devices  970 us (30%)
  other arithmetic  937 us (29%)
  matrix products  805 us (25%)
  local copies, waits for them, and re-layouts  283 us (9%)
  blocking collectives  223 us (7%)
    another operation x144, other arithmetic, block_step(): lax.linalg.triangular_solve(coupling, source, left_side=True, lower=True,...  647 us
    psum x1, waiting for transfers between devices, on_device(): lax.psum(ffn_part.astype(jnp.bfloat16), 'tp').astype(jnp.float32)  153 us
    psum x1, waiting for transfers between devices, on_device(): d_middle_norm, grad_gain_ffn = pull_second(lax.psum(d_ffn_part, 'tp'))  145 us
    psum x1, waiting for transfers between devices, on_device(): middle = tokens_f + lax.psum(attn_part, 'tp')  130 us
    dot_general x48, matrix products, block_step(): jnp.einsum('bhcd,bhmd->bhcm', k_block, memory, precision=highest_precision)  125 us
    dot_general x48, matrix products, block_step(): jnp.einsum('bhcd,bhmd->bhcm', q_block, memory, precision=highest_precision)  114 us
    dot_general x48, matrix products, block_step(): jnp.einsum('bhsm,bhsd->bhmd', weighted, k_block, precision=highest_precis...  105 us
    dot_general x48, matrix products, block_step(): jnp.einsum('bhtd,bhsd->bhts', q_block, k_block, precision=highest_precision)  75 us
  transfers between devices with their start and end apart: 22, of which 14 were waited for; matrix products, arithmetic and copies ran while one was open for 9% of the time, Pallas kernels for 0%

commit v1 on v0

v1 whole, which is shorter than its diff:
```python
from functools import partial

import jax
import jax.numpy as jnp
from jax import lax
from jax.sharding import PartitionSpec as P

BLOCK = 64


highest_precision = lax.Precision.HIGHEST
norm_epsilon = 1e-05
unit_epsilon = 1e-06
PRECISION = lax.Precision.HIGH


def from_behind(value, axis, steps):
    count = lax.axis_size(axis)
    leading, last = (max(0, -steps), min(count, count - steps))
    return lax.ppermute(value, axis, [(source, source + steps) for source in range(leading, last)])


def state_entering(last, val_dim, axis):
    count, here = (lax.axis_size(axis), lax.axis_index(axis))
    if count == 2:
        return from_behind(last[:, :, :val_dim], axis, 1)
    everything = lax.all_gather(last, axis)
    state = everything[0][:, :, :val_dim]
    state = jnp.where(here > 0, state, 0.0)
    for k in range(1, count - 1):
        new = (
            jnp.einsum(
                "bhij,bhjk->bhik", state, everything[k][:, :, val_dim:], precision=highest_precision
            )
            + everything[k][:, :, :val_dim]
        )
        state = jnp.where(k < here, new, state)
    return state


def gradient_entering(first, val_dim, axis):
    count, here = (lax.axis_size(axis), lax.axis_index(axis))
    low = first.astype(jnp.bfloat16)
    if count == 2:
        return from_behind(low[:, :, :val_dim], axis, -1).astype(jnp.float32)
    everything = lax.all_gather(low, axis).astype(jnp.float32)
    state = jnp.where(here < count - 1, everything[count - 1][:, :, :val_dim], 0.0)
    for k in range(count - 2, 0, -1):
        new = (
            jnp.einsum(
                "bhij,bhjk->bhik", state, everything[k][:, :, val_dim:], precision=highest_precision
            )
            + everything[k][:, :, :val_dim]
        )
        state = jnp.where(k > here, new, state)
    return state


def sum_over_tp(part):
    count, here = (lax.axis_size("tp"), lax.axis_index("tp"))
    low = part.astype(jnp.bfloat16)
    if count != 4:
        return lax.psum(low, "tp")
    half = part.shape[0] // 2
    even = lax.rem(here, 2) == 0
    near = [(i, i ^ 1) for i in range(count)]
    far = [(i, i ^ 2) for i in range(count)]
    keep = jnp.where(even, low[:half], low[half:])
    send = jnp.where(even, low[half:], low[:half])
    received = lax.ppermute(send, "tp", near)
    pair = (keep.astype(jnp.float32) + received.astype(jnp.float32)).astype(jnp.bfloat16)
    other = lax.ppermute(pair, "tp", far)
    total = (pair.astype(jnp.float32) + other.astype(jnp.float32)).astype(jnp.bfloat16)
    peer = lax.ppermute(total, "tp", near)
    return jnp.concatenate([jnp.where(even, total, peer), jnp.where(even, peer, total)], 0)


def summed_product(left, right, spec):
    return jnp.stack(
        [
            sum_over_tp(jnp.einsum(spec, left[b], right, preferred_element_type=jnp.float32))
            for b in range(left.shape[0])
        ]
    )


def norm_gain(values, gain):
    return values * lax.rsqrt(jnp.mean(values * values, -1, keepdims=True) + norm_epsilon) * gain


def segment_ids(positions, lengths):
    seq_ends = jnp.cumsum(lengths, axis=-1)
    return jnp.sum((seq_ends[:, None, :] <= positions[None, :, None]).astype(jnp.int32), -1)


def mm(spec, left, right):
    return jnp.einsum(spec, left, right, precision=PRECISION)


@jax.custom_vjp
def unit_lower_inverse(coupling):
    size = coupling.shape[-1]
    row = jnp.arange(size)[:, None]
    col = jnp.arange(size)[None, :]

    def off(width):
        return (
            (row // (2 * width) == col // (2 * width))
            & (row // width % 2 == 1)
            & (col // width % 2 == 0)
        )

    inverse = jnp.eye(size, dtype=jnp.float32) - jnp.where(off(1), coupling, 0.0)
    width = 2
    while width < size:
        piece = jnp.where(off(width), coupling, 0.0)
        inverse = inverse - mm(
            "nbhij,nbhjk->nbhik", mm("nbhij,nbhjk->nbhik", inverse, piece), inverse
        )
        width *= 2
    return inverse


def inverse_keep(coupling):
    inverse = unit_lower_inverse(coupling)
    return inverse, inverse


def inverse_back(inverse, grad):
    inner = mm("nbhji,nbhjk->nbhik", inverse, grad)
    return (-mm("nbhij,nbhkj->nbhik", inner, inverse),)


unit_lower_inverse.defvjp(inverse_keep, inverse_back)


def arrange(tensor):
    streams, seg_len = tensor.shape[:2]
    shaped = tensor.reshape((streams, seg_len // BLOCK, BLOCK) + tensor.shape[2:])
    return shaped.transpose((1, 0, 3, 2, 4) if tensor.ndim == 4 else (1, 0, 3, 2))


def arrange_back(tensor):
    blocks, streams, head_count, _, width = tensor.shape
    return tensor.transpose(1, 0, 3, 2, 4).reshape(streams, blocks * BLOCK, head_count, width)


def block_maps(queries, key_rows, values, log_decay, beta_gate, resets):
    q, k, v = arrange(queries), arrange(key_rows), arrange(values)
    d, b = arrange(log_decay), arrange(beta_gate)
    z = jnp.cumsum(arrange(resets[..., None]), -1)
    row = jnp.arange(BLOCK)[:, None]
    col = jnp.arange(BLOCK)[None, :]
    summed = jnp.einsum(
        "nbhs,ts->nbht", d, (row >= col).astype(jnp.float32), precision=highest_precision
    )
    inside = (z[..., :, None] == z[..., None, :]) & (row >= col)
    ratio = jnp.where(
        inside,
        jnp.exp(jnp.where(inside, summed[..., :, None] - summed[..., None, :], 0.0)),
        0.0,
    )
    from_start = jnp.where(z == 0, jnp.exp(summed), 0.0)
    gram = mm("nbhtd,nbhsd->nbhts", k, k)
    coupling = jnp.where(row > col, b[..., None] * ratio * gram, 0.0)
    inverse = unit_lower_inverse(coupling)
    wrote = mm("nbhts,nbhsv->nbhtv", inverse, b[..., None] * v)
    erased = mm("nbhts,nbhsd->nbhtd", inverse, (b * from_start)[..., None] * k)
    scores = ratio * mm("nbhtd,nbhsd->nbhts", q, k)
    offset = mm("nbhts,nbhsv->nbhtv", scores, wrote)
    reader = from_start[..., None] * q - mm("nbhts,nbhsd->nbhtd", scores, erased)
    late_keys = ratio[..., BLOCK - 1, :, None] * k
    eye = jnp.eye(k.shape[-1], dtype=jnp.float32)
    moved = from_start[..., BLOCK - 1, None, None] * eye - mm(
        "nbhtd,nbhte->nbhde", erased, late_keys
    )
    added = mm("nbhtv,nbhtd->nbhvd", wrote, late_keys)
    return moved, added, reader, offset


def run_blocks(moves, adds, spec, order):
    blocks, streams, heads, rows, width = adds.shape
    eye = jnp.broadcast_to(jnp.eye(width, dtype=jnp.float32), (streams, heads, width, width))
    memory = jnp.concatenate([jnp.zeros((streams, heads, rows, width), jnp.float32), eye], 2)
    padded = jnp.pad(adds, ((0, 0), (0, 0), (0, 0), (0, width), (0, 0)))
    states = [None] * blocks
    for n in order:
        states[n] = memory
        memory = mm(spec, memory, moves[n]) + padded[n]
    return jnp.stack(states), memory


def finish(direct, gate_raw, gain_out):
    streams, seg_len, head_count, val_dim = direct.shape
    scaled = (
        direct * lax.rsqrt(jnp.mean(direct * direct, -1, keepdims=True) + norm_epsilon) * gain_out
    )
    gated_output = scaled * jax.nn.silu(gate_raw.reshape(streams, seg_len, head_count, val_dim))
    return gated_output.reshape(streams, seg_len, head_count * val_dim)


def on_device(
    tokens,
    lengths,
    w_q,
    w_k,
    w_v,
    w_g,
    w_a,
    w_b,
    output_weight,
    w_gate,
    w_up,
    w_down,
    gain_attn,
    gain_ffn,
    gain_out,
    conv_q,
    conv_k,
    conv_v,
    a_log,
    dt_bias,
    d_out,
):
    shards = ("dp", "ctx")
    shard_count = lax.axis_size(shards)
    shard_rows = w_q.shape[0]
    gain_rows = gain_out.shape[0]
    first_pack = jnp.concatenate(
        [
            w_q,
            w_k,
            w_v,
            w_g,
            w_a,
            w_b,
            gain_attn[:, None],
            gain_ffn[:, None],
            jnp.pad(gain_out, (0, shard_rows - gain_rows))[:, None],
        ],
        1,
    )
    w_first = lax.all_gather(first_pack, shards, axis=0, tiled=True)
    second_pack = jnp.concatenate([output_weight, w_gate, w_up, w_down], 1)
    second_pack, w_first = lax.optimization_barrier((second_pack, w_first))
    w_second = lax.all_gather(second_pack, shards, axis=0, tiled=True)
    streams, seg_len = (tokens.shape[0], tokens.shape[1])
    head_count = a_log.shape[0]
    key_cols = w_q.shape[1]
    val_cols = w_v.shape[1]
    key_dim = key_cols // head_count
    val_dim = val_cols // head_count
    hidden_cols = w_gate.shape[1]
    conv_width = conv_q.shape[0]
    mixed_cols = 2 * key_cols + val_cols
    halo_rows = conv_width - 1
    positions = (
        lax.axis_index("ctx") * seg_len
        - halo_rows
        + jnp.arange(seg_len + halo_rows, dtype=jnp.int32)
    )
    segment = segment_ids(positions, lengths)
    own_segment = segment[:, halo_rows:]
    tap_masks = [
        (
            (segment[:, offset : offset + seg_len] == own_segment)
            & (positions[offset : offset + seg_len] >= 0)[None, :]
        ).astype(jnp.float32)[..., None]
        for offset in range(conv_width)
    ]
    keep_mask = (own_segment == segment[:, halo_rows - 1 : halo_rows - 1 + seg_len]) & (
        positions[halo_rows:] > 0
    )[None, :]
    resets = 1 - keep_mask.astype(jnp.int32)
    tokens_f = tokens.astype(jnp.float32)
    main_cols = mixed_cols + val_cols
    side_cols_all = 2 * head_count
    gains = w_first[:, main_cols + side_cols_all :].astype(jnp.float32)
    gain_attn_f = gains[:, 0]
    gain_ffn_f = gains[:, 1]
    gain_out_f = gains[:, 2].reshape(shard_count, shard_rows)[:, :gain_rows].reshape(-1)
    w_main = w_first[:, :main_cols]
    w_side = w_first[:, main_cols : main_cols + side_cols_all]
    w_o = w_second[:, :val_cols]
    w_pair = w_second[:, val_cols : val_cols + 2 * hidden_cols]
    w_back = w_second[:, val_cols + 2 * hidden_cols :]
    normed = norm_gain(tokens_f, gain_attn_f).astype(jnp.bfloat16)
    projected = jnp.einsum("bsd,dc->bsc", normed, w_main, preferred_element_type=jnp.float32)
    mixed_raw = projected[..., :mixed_cols].astype(jnp.bfloat16)
    gate_raw = projected[..., mixed_cols:]
    side_raw = jnp.einsum("bsd,dc->bsc", normed, w_side, preferred_element_type=jnp.float32)
    halo = from_behind(mixed_raw[:, seg_len - halo_rows :], "ctx", 1)
    raw_ext = jnp.concatenate([halo, mixed_raw], 1).astype(jnp.float32)
    conv_all = jnp.concatenate([conv_q, conv_k, conv_v], 1).astype(jnp.float32)

    def prepare(raw_cols, side_cols, conv_weight, log_rate, rate_bias):
        summed = raw_cols[:, 0:seg_len] * conv_weight[0] * tap_masks[0]
        for offset in range(1, conv_width):
            summed = (
                summed
                + raw_cols[:, offset : offset + seg_len] * conv_weight[offset] * tap_masks[offset]
            )
        active = jax.nn.silu(summed)
        queries = active[..., :key_cols].reshape(streams, seg_len, head_count, key_dim)
        key_rows = active[..., key_cols : 2 * key_cols].reshape(
            streams, seg_len, head_count, key_dim
        )
        values = active[..., 2 * key_cols :].reshape(streams, seg_len, head_count, val_dim)
        queries = (
            queries
            * lax.rsqrt(jnp.sum(queries * queries, -1, keepdims=True) + unit_epsilon)
            * key_dim ** (-0.5)
        )
        key_rows = key_rows * lax.rsqrt(
            jnp.sum(key_rows * key_rows, -1, keepdims=True) + unit_epsilon
        )
        log_decay = -jnp.exp(log_rate) * jax.nn.softplus(side_cols[..., :head_count] + rate_bias)
        beta_gate = jax.nn.sigmoid(side_cols[..., head_count:])
        return (queries, key_rows, values, log_decay, beta_gate)

    prepared, pull_prepare = jax.vjp(prepare, raw_ext, side_raw, conv_all, a_log, dt_bias)
    maps, pull_maps = jax.vjp(partial(block_maps, resets=resets), *prepared)
    moved, added, reader, offset = maps
    before, last = run_blocks(
        moved, added, "bhij,bhjk->bhik", range(seg_len // BLOCK)
    )
    state_in = state_entering(last, val_dim, "ctx")
    states = before[:, :, :, :val_dim] + mm(
        "bhvd,nbhde->nbhve", state_in, before[:, :, :, val_dim:]
    )
    direct = arrange_back(offset + mm("nbhtd,nbhvd->nbhtv", reader, states))
    gated_f, pull_finish = jax.vjp(finish, direct, gate_raw, gain_out_f)
    gated = gated_f.astype(jnp.bfloat16)
    middle = tokens_f + summed_product(gated, w_o, "sc,dc->sd").astype(jnp.float32)
    normed_full, pull_second = jax.vjp(norm_gain, middle, gain_ffn_f)
    normed_ffn = normed_full.astype(jnp.bfloat16)
    paired = jnp.einsum("bsd,dc->bsc", normed_ffn, w_pair, preferred_element_type=jnp.float32)
    gate_val = paired[..., :hidden_cols]
    up_val = paired[..., hidden_cols:]
    hidden = (jax.nn.silu(gate_val) * up_val).astype(jnp.bfloat16)
    layer_out = (middle + summed_product(hidden, w_back, "sf,df->sd").astype(jnp.float32)).astype(
        jnp.bfloat16
    )
    cotangent = d_out.astype(jnp.float32)
    d_hidden = jnp.einsum("bsd,df->bsf", d_out, w_back, preferred_element_type=jnp.float32)
    grad_down = jnp.einsum("bsd,bsf->df", d_out, hidden, preferred_element_type=jnp.float32)
    sig_gate = jax.nn.sigmoid(gate_val)
    d_gate = (d_hidden * up_val * sig_gate * (1.0 + gate_val * (1.0 - sig_gate))).astype(
        jnp.bfloat16
    )
    d_up = (d_hidden * gate_val * sig_gate).astype(jnp.bfloat16)
    d_paired = jnp.concatenate([d_gate, d_up], -1)
    grad_pair = jnp.einsum("bsd,bsc->dc", normed_ffn, d_paired, preferred_element_type=jnp.float32)
    d_normed_ffn = summed_product(d_paired, w_pair, "sc,dc->sd").astype(jnp.float32)
    d_middle_norm, grad_gain_ffn = pull_second(d_normed_ffn)
    d_middle = cotangent + d_middle_norm
    d_attention = d_middle.astype(jnp.bfloat16)
    grad_out_proj = jnp.einsum(
        "bsd,bsc->dc", d_attention, gated, preferred_element_type=jnp.float32
    )
    d_gated = jnp.einsum(
        "bsd,dc->bsc", d_attention, w_o, preferred_element_type=jnp.float32
    )
    early_pack = jnp.concatenate(
        [grad_out_proj, grad_pair, grad_down, grad_gain_ffn[:, None]], 1
    ).astype(jnp.bfloat16)
    early = lax.psum_scatter(early_pack, shards, scatter_dimension=0, tiled=True).astype(
        jnp.float32
    )
    d_direct, d_gate_raw, grad_gain_out = pull_finish(d_gated)
    d_offset = arrange(d_direct)
    d_states = mm("nbhtv,nbhtd->nbhvd", d_offset, reader)
    after, first = run_blocks(
        moved, d_states, "bhij,bhkj->bhik", range(seg_len // BLOCK - 1, -1, -1)
    )
    d_state_out = gradient_entering(first, val_dim, "ctx")
    d_added = after[:, :, :, :val_dim] + mm(
        "bhvd,nbhde->nbhve", d_state_out, after[:, :, :, val_dim:]
    )
    d_moved = mm("nbhvd,nbhve->nbhde", states, d_added)
    d_reader = mm("nbhtv,nbhvd->nbhtd", d_offset, states)
    d_prepared = pull_maps((d_moved, d_added, d_reader, d_offset))
    d_raw_ext, d_side, d_conv, d_log_rate, d_rate_bias = pull_prepare(d_prepared)
    returned = from_behind(d_raw_ext[:, :halo_rows], "ctx", -1)
    d_raw = d_raw_ext[:, halo_rows:]
    d_raw = jnp.concatenate(
        [d_raw[:, : seg_len - halo_rows], d_raw[:, seg_len - halo_rows :] + returned], 1
    )
    d_projected = jnp.concatenate([d_raw, d_gate_raw], -1).astype(jnp.bfloat16)
    d_side_low = d_side.astype(jnp.bfloat16)
    grad_main = jnp.einsum("bsd,bsc->dc", normed, d_projected, preferred_element_type=jnp.float32)
    grad_side = jnp.einsum("bsd,bsc->dc", normed, d_side_low, preferred_element_type=jnp.float32)
    late_pack = jnp.concatenate([grad_main, grad_side], 1).astype(jnp.bfloat16)
    late = lax.psum_scatter(late_pack, shards, scatter_dimension=0, tiled=True).astype(jnp.float32)
    d_all = jnp.concatenate([d_projected, d_side_low], -1)
    d_normed = summed_product(
        d_all, w_first[:, : main_cols + side_cols_all], "sc,dc->sd"
    ).astype(jnp.float32)
    recomputed, pull_first = jax.vjp(norm_gain, tokens_f, gain_attn_f)
    d_tokens_norm, grad_gain_attn = pull_first(d_normed)
    grad_tokens = d_middle + d_tokens_norm
    grad_gain_out = lax.psum(grad_gain_out, "tp")
    pieces = (d_conv, d_log_rate, d_rate_bias, grad_gain_attn, grad_gain_out)
    flat = lax.psum(jnp.concatenate([piece.reshape(-1) for piece in pieces]), shards)
    sums, place = ([], 0)
    for piece in pieces:
        sums.append(flat[place : place + piece.size].reshape(piece.shape))
        place += piece.size
    shard = lax.axis_index(shards)
    own_attn = lax.dynamic_slice_in_dim(sums[3], shard * shard_rows, shard_rows)
    own_out = lax.dynamic_slice_in_dim(sums[4], shard * gain_rows, gain_rows)
    pair_end = val_cols + 2 * hidden_cols
    down_end = pair_end + hidden_cols
    return (
        layer_out,
        grad_tokens,
        late[:, :key_cols],
        late[:, key_cols : 2 * key_cols],
        late[:, 2 * key_cols : mixed_cols],
        late[:, mixed_cols:main_cols],
        late[:, main_cols : main_cols + head_count],
        late[:, main_cols + head_count :],
        early[:, :val_cols],
        early[:, val_cols : val_cols + hidden_cols],
        early[:, val_cols + hidden_cols : pair_end],
        early[:, pair_end:down_end],
        own_attn,
        early[:, down_end],
        own_out,
        sums[0][:, :key_cols],
        sums[0][:, key_cols : 2 * key_cols],
        sums[0][:, 2 * key_cols :],
        sums[1],
        sums[2],
    )


def solution(mesh):
    return jax.shard_map(
        on_device,
        mesh=mesh,
        in_specs=(
            P("dp", "ctx", None),
            P("dp", None),
            P(("dp", "ctx"), "tp"),
            P(("dp", "ctx"), "tp"),
            P(("dp", "ctx"), "tp"),
            P(("dp", "ctx"), "tp"),
            P(("dp", "ctx"), "tp"),
            P(("dp", "ctx"), "tp"),
            P(("dp", "ctx"), "tp"),
            P(("dp", "ctx"), "tp"),
            P(("dp", "ctx"), "tp"),
            P(("dp", "ctx"), "tp"),
            P(("dp", "ctx")),
            P(("dp", "ctx")),
            P(("dp", "ctx")),
            P(None, "tp"),
            P(None, "tp"),
            P(None, "tp"),
            P("tp"),
            P("tp"),
            P("dp", "ctx", None),
        ),
        out_specs=(
            P("dp", "ctx", None),
            P("dp", "ctx", None),
            P(("dp", "ctx"), "tp"),
            P(("dp", "ctx"), "tp"),
            P(("dp", "ctx"), "tp"),
            P(("dp", "ctx"), "tp"),
            P(("dp", "ctx"), "tp"),
            P(("dp", "ctx"), "tp"),
            P(("dp", "ctx"), "tp"),
            P(("dp", "ctx"), "tp"),
            P(("dp", "ctx"), "tp"),
            P(("dp", "ctx"), "tp"),
            P(("dp", "ctx")),
            P(("dp", "ctx")),
            P(("dp", "ctx")),
            P(None, "tp"),
            P(None, "tp"),
            P(None, "tp"),
            P("tp"),
            P("tp"),
        ),
        check_vma=False,
    )
```

time: 3260 us -> 969 us (0.30)
  waiting for transfers between devices: 970 us -> 154 us
  other arithmetic: 937 us -> 171 us
  matrix products: 805 us -> 311 us
  blocking collectives: 223 us -> 77.4 us
  local copies, waits for them, and re-layouts: 283 us -> 204 us
    another operation x211 -> x10, other arithmetic: 683 us -> 11 us  [the longest x144 647 us: block_step(): lax.linalg.triangular_solve(coupling, source, left_side=True, lower=True,...]
    psum x3 -> x0, waiting for transfers between devices: 429 us -> none  [the longest x1 153 us: on_device(): lax.psum(ffn_part.astype(jnp.bfloat16), 'tp').astype(jnp.float32)]
    reduce_scatter x8 -> x2, waiting for transfers between devices: 417 us -> 0.01 us  [the longest x1 0.01 us: on_device(): lax.psum_scatter(late_pack, shards, scatter_dimension=0, tiled=True)]
    dot_general x318 -> x86, matrix products: 659 us -> 253 us  [the longest x72 201 us: mm(): return jnp.einsum(spec, left, right, precision=PRECISION)]
    all_gather x9 -> x0, blocking collectives: 161 us -> none  [the longest x1 32.5 us: on_device(): lax.all_gather(w_q, ('dp', 'ctx'), axis=0, tiled=True)]
    ppermute x0 -> x24, waiting for transfers between devices: none -> 98.3 us  [the longest x8 94.9 us: sum_over_tp(): other = lax.ppermute(pair, 'tp', far)]
    another operation x48 -> x0, matrix products: 74.1 us -> none  [block_step(): lax.linalg.triangular_solve(coupling, source, left_side=True, lower=True,...]
    psum x1 -> x2, blocking collectives: 6.28 us -> 77.4 us  [the longest x1 41.1 us: on_device(): grad_gain_out = lax.psum(grad_gain_out, 'tp')]
  transfers between devices with their start and end apart: 22 -> 32, of which waited for: 14 -> 10; matrix products, arithmetic and copies ran while one was open for 9% -> 36% of each run, Pallas kernels for 0% -> 0%
where the time goes in v1:
time: 969 us; the launch traced here: 960 us
  matrix products  311 us (32%)
  local copies, waits for them, and re-layouts  204 us (21%)
  other arithmetic  171 us (18%)
  waiting for transfers between devices  154 us (16%)
  blocking collectives  77.4 us (8%)
  starting transfers between devices  25.3 us (3%)
  between operations  17.4 us (2%)
    dot_general x72, matrix products, mm(): return jnp.einsum(spec, left, right, precision=PRECISION)  201 us
    ppermute x8, waiting for transfers between devices, sum_over_tp(): other = lax.ppermute(pair, 'tp', far)  94.9 us
    all_gather x1, waiting for transfers between devices, on_device(): w_first = lax.all_gather(first_pack, shards, axis=0, tiled=True)  53.5 us
    unnamed x369, local copies, waits for them, and re-layouts  43.4 us
    psum x1, blocking collectives, on_device(): grad_gain_out = lax.psum(grad_gain_out, 'tp')  41.1 us
    psum x1, blocking collectives, on_device(): lax.psum(jnp.concatenate([piece.reshape(-1) for piece in pieces]), shards)  36.4 us
    dot_general x8, matrix products, summed_product(): jnp.einsum(spec, left[b], right, preferred_element_type=jnp.float32)  30.1 us
  transfers between devices with their start and end apart: 32, of which 10 were waited for; matrix products, arithmetic and copies ran while one was open for 36% of the time, Pallas kernels for 0%

profile of v1, /device:TPU:0, one launch (start us, length us, event | category | flops | bytes accessed | tf_op | source)
XLA Modules:
  0.0 960.4 jit_solution(1212722620165262813)
XLA Ops:
  28.5 53.5 %all-gather.3.cloned.1.call-done = bf16[1024,1543]{0,1:T(8,128)(2,1)} async-done(((bf16[128,1543]{0,1:T(8,128)(2,1)}), bf16[1024,1543]{0,1:T(8,128)(2,1)}) %all-gather.3.cloned.1.call-update) | async-done | bytes 3160080 | tf_op jit(solution)/shard_map/all_gather | solution.py:243
  88.5 12.6 %fusion.348 = (bf16[2,1024,1536]{2,1,0:T(8,128)(2,1)S(1)}, f32[2,1024,1536]{2,1,0:T(8,128)}) fusion(bf16[1024,1543]{0,1:T(8,128)(2,1)} %all-gather.3.cloned.1.call-done, bf16[2,1024,1024]{2,1,0:T(8,128)(2,1)} %param.21, f32[1024]{0:T(1024)S(1)} %bitcast.679, f32[2,1024]{1,0:T(2,128)S(1)} %fusion.302), kind=kOutput, calls=%fused_computation.668 | convolution fusion | flops 6453985280 | bytes 26226688 | tf_op jit(solution)/shard_map/bsd,dc->bsc/dot_general | solution.py:288
  112.7 8.3 fusion.14
  135.8 5.9 reshape.1025
  141.7 5.0 multiply_reduce_fusion.10
  176.9 4.9 multiply_reduce_fusion.11
  190.3 10.6 %fusion.137 = f32[16,2,2,256,128]{4,3,2,1,0:T(8,128)} fusion(f32[16,2,2,64,256]{4,3,2,1,0:T(8,128)S(1)} %fusion.43, f32[16,2,2,64]{3,2,1,0:T(2,128)S(1)} %bitcast.662, f32[2,16,64,2,128]{4,3,2,1,0:T(2,128)S(1)} %reshape.1022, f32[2,16,64,2]{2,3,0,1:T(2,128)S(1)} %copy.452), kind=kOutput, calls=%fused_computation.274 | convolution fusion | flops 806354944 | bytes 14712832 | tf_op jit(solution)/shard_map/jvp(nbhtv,nbhtd->nbhvd)/dot_general | solution.py:97
  206.3 5.2 multiply_subtract_fusion
  247.9 7.8 slice_add_fusion.1
  255.7 6.3 multiply_reduce_fusion.8
  266.3 6.4 mul.777
  272.7 7.5 copy.463
  280.2 6.8 reshape.1026
  287.0 6.3 multiply_convert_fusion.2
  303.3 22.9 %collective-permute-done.6 = bf16[512,1024]{1,0:T(8,128)(2,1)S(1)} collective-permute-done((bf16[512,1024]{1,0:T(8,128)(2,1)S(1)}, bf16[512,1024]{1,0:T(8,128)(2,1)S(1)}, u32[]{:S(2)}, u32[]{:S(2)}) %collective-permute-start.6) | collective-permute-done | bytes 1048608 | tf_op jit(solution)/shard_map/ppermute | solution.py:72
  326.7 21.2 %collective-permute-done.3 = bf16[512,1024]{1,0:T(8,128)(2,1)S(1)} collective-permute-done((bf16[512,1024]{1,0:T(8,128)(2,1)S(1)}, bf16[512,1024]{1,0:T(8,128)(2,1)S(1)}, u32[]{:S(2)}, u32[]{:S(2)}) %collective-permute-start.3) | collective-permute-done | bytes 1048608 | tf_op jit(solution)/shard_map/ppermute | solution.py:72
  353.3 9.6 fusion.63
  362.9 10.6 %fusion.25 = (bf16[2,1024,704]{2,1,0:T(8,128)(2,1)S(1)}, bf16[2,1024,704]{2,1,0:T(8,128)(2,1)}, bf16[2,1024,704]{2,1,0:T(8,128)(2,1)}) fusion(f32[2,1024,1408]{2,1,0:T(8,128)} %fusion.63, bf16[2,1024,1024]{2,1,0:T(8,128)(2,1)S(1)} %copy-done.55, bf16[1024,2624]{1,0:T(8,128)(2,1)S(1)} %copy-done.158), kind=kOutput, calls=%fused_computation.95 | convolution fusion | flops 2975858688 | bytes 25952256 | tf_op jit(solution)/shard_map/bsd,df->bsf/dot_general | solution.py:345
  373.5 6.0 fusion.130
  389.1 21.8 %collective-permute-done.15 = bf16[512,1024]{1,0:T(8,128)(2,1)S(1)} collective-permute-done((bf16[512,1024]{1,0:T(8,128)(2,1)S(1)}, bf16[512,1024]{1,0:T(8,128)(2,1)S(1)}, u32[]{:S(2)}, u32[]{:S(2)}) %collective-permute-start.15) | collective-permute-done | bytes 1048608 | tf_op jit(solution)/shard_map/ppermute | solution.py:72
  412.3 20.6 %collective-permute-done.18 = bf16[512,1024]{1,0:T(8,128)(2,1)S(1)} collective-permute-done((bf16[512,1024]{1,0:T(8,128)(2,1)S(1)}, bf16[512,1024]{1,0:T(8,128)(2,1)S(1)}, u32[]{:S(2)}, u32[]{:S(2)}) %collective-permute-start.18) | collective-permute-done | bytes 1048608 | tf_op jit(solution)/shard_map/ppermute | solution.py:72
  436.1 5.5 mul.826
  466.1 5.8 fusion.32
  471.8 5.9 reshape.1027
  477.7 5.9 reshape.1028
  483.6 6.8 multiply_reduce_fusion.5
  496.4 5.9 fusion.90
  502.3 7.6 fusion.349
  540.1 10.7 %slice_add_fusion = f32[16,2,2,256,128]{4,3,2,1,0:T(8,128)} fusion(f32[16,2,2,384,128]{4,3,2,1,0:T(8,128)} %fusion.183, bf16[2,2,256,128]{3,2,1,0:T(8,128)(2,1)S(1)} %collective-permute-done.20), kind=kOutput, calls=%fused_computation.60 | convolution fusion | flops 1612709888 | bytes 21233664 | tf_op jit(solution)/shard_map/bhvd,nbhde->nbhve/dot_general | solution.py:97
  550.8 14.6 %multiply_reduce_fusion.6 = (f32[16,2,2]{2,1,0:T(2,128)S(1)}, f32[16,2,2,128,128]{4,3,2,1,0:T(8,128)}) fusion(f32[128,128]{1,0:T(8,128)S(1)} %copy-done.88, f32[16,2,2,256,128]{4,3,2,1,0:T(8,128)} %copy-done.10, f32[16,2,2,256,128]{4,3,2,1,0:T(8,128)} %slice_add_fusion), kind=kOutput, calls=%fused_computation.120 | convolution fusion | flops 1612709888 | bytes 21037312 | tf_op jit(solution)/shard_map/nbhvd,nbhve->nbhde/dot_general | solution.py:97
  565.5 8.3 fusion.350
  573.8 5.6 fusion.136
  619.6 7.0 bitcast_add_fusion.1
  656.2 5.3 copy.481
  661.5 6.4 reshape.1029
  667.9 7.2 add_add_fusion.4
  676.3 12.0 %multiply_reduce_fusion.3 = (f32[1024]{0:T(1024)S(1)}, f32[1024]{0:T(1024)S(1)}, f32[1024]{0:T(1024)S(1)}, f32[1024]{0:T(1024)S(1)}, f32[2,1024,1024]{2,1,0:T(8,128)}) fusion(f32[2,1027,1024]{2,1,0:T(8,128)S(1)} %bitcast.658, f32[1024]{0:T(1024)S(1)} %copy-done.131, f32[2,1024]{1,0:T(2,128)S(1)} %copy-done.118, f32[2,1024]{1,0:T(2,128)S(1)} %copy-done.116, ...), kind=kLoop, calls=%fused_computation.65 | loop fusion | flops 48230400 | bytes 58765312 | tf_op jit(solution)/shard_map/transpose(jvp())/reduce_sum | solution.py:301
  688.4 10.2 %multiply_multiply_fusion.3 = (f32[2,1024,1024]{2,1,0:T(8,128)S(1)}, f32[2,1024,1024]{2,1,0:T(8,128)S(1)}, f32[2,1024,1024]{2,1,0:T(8,128)}, f32[2,1024,1024]{2,1,0:T(8,128)}) fusion(f32[2,1024,1024]{2,1,0:T(8,128)} %get-tuple-element.160, f32[1024]{0:T(1024)S(1)} %copy-done.131, f32[1024]{0:T(1024)S(1)} %bitcast.687, f32[1024]{0:T(1024)S(1)} %bitcast.685, ...), kind=kLoop, calls=%fused_computation.75 | loop fusion | flops 16777216 | bytes 41988096 | tf_op jit(solution)/shard_map/transpose(jvp())/mul | solution.py:301
  704.6 12.5 %pad_add_fusion = bf16[2,1027,1024]{2,1,0:T(8,128)(2,1)} fusion(f32[2,1024,1024]{2,1,0:T(8,128)} %copy-done.12, f32[2,1024,1024]{2,1,0:T(8,128)} %get-tuple-element.179, f32[2,1024,1024]{2,1,0:T(8,128)} %get-tuple-element.180, f32[2,1024,1024]{2,1,0:T(8,128)S(1)} %get-tuple-element.177), kind=kLoop, calls=%fused_computation.48 | loop fusion | flops 8413184 | bytes 37761024 | tf_op jit(solution)/shard_map/transpose(jvp())/add_any | solution.py:297
  731.8 7.4 bitcast_convert_fusion
  741.2 6.3 fusion.159
  758.6 12.4 %bitcast_convert_fusion.1 = bf16[1024,1408]{1,0:T(8,128)(2,1)} fusion(bf16[2,1024,704]{2,1,0:T(8,128)(2,1)} %copy-done.162, bf16[2,1024,704]{2,1,0:T(8,128)(2,1)} %get-tuple-element.171, bf16[2,1024,1024]{2,1,0:T(8,128)(2,1)S(1)} %copy-done.7, f32[1024]{0:T(1024)S(1)} %bitcast.672, f32[2,1024]{1,0:T(2,128)S(1)} %copy-done.109, ...), kind=kOutput, calls=%fused_computation.101 | convolution fusion | flops 5933236224 | bytes 17051648 | tf_op jit(solution)/shard_map/bsd,bsc->dc/dot_general | solution.py:353
  783.2 9.3 concatenate.84
  793.6 6.0 pad_maximum_fusion.1
  813.7 8.4 collective-permute-done.9
  828.2 41.1 %psum.14 = f32[256]{0:T(256)S(1)} all-reduce(f32[256]{0:T(256)S(1)} %copy-done.149), channel_id=1, replica_groups=mesh['dp'=4,'ctx'=2,'tp'=4] {'tp'}, use_global_device_ids=true, to_apply=%region_32.33 | all-reduce | flops 256 | bytes 2048 | tf_op jit(solution)/shard_map/psum | solution.py:402
  887.0 36.4 %psum.15 = f32[5380]{0:T(1024)S(1)} all-reduce(f32[5380]{0:T(1024)S(1)} %concatenate.85), channel_id=1, replica_groups=mesh['dp'=4,'ctx'=2,'tp'=4] {'dp','ctx'}, use_global_device_ids=true, to_apply=%region_33.34 | all-reduce | flops 5380 | bytes 43040 | tf_op jit(solution)/shard_map/psum | solution.py:404
  926.5 16.0 %fusion.11 = (f32[2,1024,1024]{2,1,0:T(8,128)}, bf16[2,1024,1024]{2,1,0:T(8,128)(2,1)}) fusion(bf16[2,1024,1024]{2,1,0:T(8,128)(2,1)} %param.21, f32[2,1024]{1,0:T(2,128)S(1)} %multiply_multiply_fusion.7, f32[1024]{0:T(1024)S(1)} %bitcast.683, f32[2,1024]{1,0:T(2,128)S(1)} %copy-done.122, f32[2,1024]{1,0:T(2,128)S(1)} %copy-done.120, ...), kind=kLoop, calls=%fused_computation.56 | loop fusion | flops 52428800 | bytes 37789696 | tf_op jit(solution)/shard_map/add | solution.py:401
  (707 shorter events, 396.7 us)
Async XLA Ops:
  7.2 74.8 %all-gather.3.cloned.1.call-start = ((), (), s32[]{:S(2)}) async-start(), calls=%async_computation.2 | async-start | bytes 3557376 | tf_op jit(solution)/shard_map/all_gather | solution.py:243
  15.9 277.5 %all-gather.5.cloned.1.call-start = ((), (), s32[]{:S(2)}) async-start(), calls=%async_computation.3 | async-start | bytes 6193152 | tf_op jit(solution)/shard_map/all_gather | solution.py:246
  16.9 95.7 %copy-start.130 = (f32[1024]{0:T(1024)}, f32[1024]{0:T(1024)S(1)}, u32[]{:S(2)}) copy-start(f32[1024]{0:T(1024)S(1)} %get-tuple-element.233) | copy-start | bytes 12292
  22.9 146.1 %copy-start.144 = (pred[64,64]{1,0:T(8,128)(4,1)}, pred[64,64]{1,0:T(8,128)(4,1)S(1)}, u32[]{:S(2)}) copy-start(pred[64,64]{1,0:T(8,128)(4,1)S(1)} %iota_compare_fusion.1) | copy-start | bytes 12292
  23.0 182.8 %copy-start.87 = (f32[128,128]{1,0:T(8,128)}, f32[128,128]{1,0:T(8,128)S(1)}, u32[]{:S(2)}) copy-start(f32[128,128]{1,0:T(8,128)S(1)} %fusion.270) | copy-start | bytes 196612
  23.0 188.5 %copy-start.71 = (f32[2,2,128,128]{3,2,1,0:T(8,128)}, f32[2,2,128,128]{3,2,1,0:T(8,128)S(1)}, u32[]{:S(2)}) copy-start(f32[2,2,128,128]{3,2,1,0:T(8,128)S(1)} %broadcast_in_dim.179) | copy-start | bytes 786436
  28.0 84.6 %copy-start.136 = (f32[1,1024]{1,0:T(1,128)}, f32[1,1024]{1,0:T(1,128)S(1)}, u32[]{:S(2)}) copy-start(f32[1,1024]{1,0:T(1,128)S(1)} %get-tuple-element.222) | copy-start | bytes 12292
  28.0 84.6 %copy-start.138 = (f32[1,1024]{1,0:T(1,128)}, f32[1,1024]{1,0:T(1,128)S(1)}, u32[]{:S(2)}) copy-start(f32[1,1024]{1,0:T(1,128)S(1)} %get-tuple-element.223) | copy-start | bytes 12292
  28.0 84.6 %copy-start.140 = (f32[1,1024]{1,0:T(1,128)}, f32[1,1024]{1,0:T(1,128)S(1)}, u32[]{:S(2)}) copy-start(f32[1,1024]{1,0:T(1,128)S(1)} %get-tuple-element.224) | copy-start | bytes 12292
  28.0 84.6 %copy-start.142 = (f32[1,1024]{1,0:T(1,128)}, f32[1,1024]{1,0:T(1,128)S(1)}, u32[]{:S(2)}) copy-start(f32[1,1024]{1,0:T(1,128)S(1)} %get-tuple-element.225) | copy-start | bytes 12292
  28.2 84.5 %copy-start.113 = (f32[2,1024]{1,0:T(2,128)}, f32[2,1024]{1,0:T(2,128)S(1)}, u32[]{:S(2)}) copy-start(f32[2,1024]{1,0:T(2,128)S(1)} %get-tuple-element.229) | copy-start | bytes 24580
  28.5 214.8 %copy-start.49 = (pred[16,2,64,64]{3,2,1,0:T(8,128)(4,1)}, pred[16,2,64,64]{3,2,1,0:T(8,128)(4,1)S(1)}, u32[]{:S(2)}) copy-start(pred[16,2,64,64]{3,2,1,0:T(8,128)(4,1)S(1)} %compare_and_fusion) | copy-start | bytes 393220
  103.7 838.8 %reduce-scatter.3.cloned.1.call-start = ((), (), s32[]{:S(2)}) async-start(), calls=%async_computation.4 | async-start | bytes 3833856 | tf_op jit(solution)/shard_map/reduce_scatter | solution.py:394
  103.9 139.5 %copy-start.59 = (f32[16,2,2,64]{3,2,1,0:T(2,128)}, f32[16,2,2,64]{3,2,1,0:T(2,128)S(1)}, u32[]{:S(2)}) copy-start(f32[16,2,2,64]{3,2,1,0:T(2,128)S(1)} %copy.445) | copy-start | bytes 49156
  103.9 4.9 collective-permute-start
  108.8 97.0 %copy-start.82 = (f32[16,2,2,1,64]{4,3,2,1,0:T(1,128)}, f32[16,2,2,1,64]{4,3,2,1,0:T(1,128)S(1)}, u32[]{:S(2)}) copy-start(f32[16,2,2,1,64]{4,3,2,1,0:T(1,128)S(1)} %slice.622) | copy-start | bytes 49156
  131.8 105.5 %copy-start.2 = (f32[2,16,64,2,128]{4,3,2,1,0:T(2,128)}, f32[2,16,64,2,128]{4,3,2,1,0:T(2,128)S(1)}, u32[]{:S(2)}) copy-start(f32[2,16,64,2,128]{4,3,2,1,0:T(2,128)S(1)} %reshape.1022) | copy-start | bytes 6291460
  149.6 87.8 %copy-start.77 = (f32[2,16,64,2]{2,3,0,1:T(2,128)}, f32[2,16,64,2]{2,3,0,1:T(2,128)S(1)}, u32[]{:S(2)}) copy-start(f32[2,16,64,2]{2,3,0,1:T(2,128)S(1)} %copy.452) | copy-start | bytes 49156
  233.3 14.6 %collective-permute-start.1 = (f32[2,2,256,128]{3,2,1,0:T(8,128)S(1)}, f32[2,2,256,128]{3,2,1,0:T(8,128)S(1)}, u32[]{:S(2)}, u32[]{:S(2)}) collective-permute-start(f32[2,2,256,128]{3,2,1,0:T(8,128)S(1)} %slice_add_fusion.3), channel_id=1, source_target_pairs={{0,4},{1,5},{2,6},{3,7},{8,12},{9,13},{10,14},{11,15},{16,20},{17,... | collective-permute-start | bytes 1572872 | tf_op jit(solution)/shard_map/ppermute | solution.py:20
  296.8 2.7 collective-permute-start.5
  298.4 3.3 collective-permute-start.2
  300.2 26.1 %collective-permute-start.6 = (bf16[512,1024]{1,0:T(8,128)(2,1)S(1)}, bf16[512,1024]{1,0:T(8,128)(2,1)S(1)}, u32[]{:S(2)}, u32[]{:S(2)}) collective-permute-start(bf16[512,1024]{1,0:T(8,128)(2,1)S(1)} %add_convert_fusion.14), channel_id=1, source_target_pairs={{0,2},{1,3},{2,0},{3,1},{4,6},{5,7},{6,4},{7,5},{8,10},{9,11},{10,... | collective-permute-start | bytes 3145736 | tf_op jit(solution)/shard_map/ppermute | solution.py:72
  302.4 45.5 %collective-permute-start.3 = (bf16[512,1024]{1,0:T(8,128)(2,1)S(1)}, bf16[512,1024]{1,0:T(8,128)(2,1)S(1)}, u32[]{:S(2)}, u32[]{:S(2)}) collective-permute-start(bf16[512,1024]{1,0:T(8,128)(2,1)S(1)} %add_convert_fusion.16), channel_id=1, source_target_pairs={{0,2},{1,3},{2,0},{3,1},{4,6},{5,7},{6,4},{7,5},{8,10},{9,11},{10,... | collective-permute-start | bytes 3145736 | tf_op jit(solution)/shard_map/ppermute | solution.py:72
  326.7 21.7 %collective-permute-start.7 = (bf16[512,1024]{1,0:T(8,128)(2,1)S(1)}, bf16[512,1024]{1,0:T(8,128)(2,1)S(1)}, u32[]{:S(2)}, u32[]{:S(2)}) collective-permute-start(bf16[512,1024]{1,0:T(8,128)(2,1)S(1)} %add_convert_fusion.13), channel_id=1, source_target_pairs={{0,1},{1,0},{2,3},{3,2},{4,5},{5,4},{6,7},{7,6},{8,9},{9,8},{10,11... | collective-permute-start | bytes 3145736 | tf_op jit(solution)/shard_map/ppermute | solution.py:74
  348.3 2.7 collective-permute-start.4
  348.7 107.4 %copy-start.27 = (bf16[1,1024,1024]{2,1,0:T(8,128)(2,1)}, bf16[1,1024,1024]{2,1,0:T(8,128)(2,1)S(1)}, u32[]{:S(2)}) copy-start(bf16[1,1024,1024]{2,1,0:T(8,128)(2,1)S(1)} %maximum_bitcast_fusion.1) | copy-start | bytes 6291460
  353.3 102.9 %copy-start.108 = (f32[2,1024]{1,0:T(2,128)}, f32[2,1024]{1,0:T(2,128)S(1)}, u32[]{:S(2)}) copy-start(f32[2,1024]{1,0:T(2,128)S(1)} %fusion.303) | copy-start | bytes 24580
  379.7 4.5 collective-permute-start.14
  384.1 2.7 collective-permute-start.17
  384.9 26.0 %collective-permute-start.15 = (bf16[512,1024]{1,0:T(8,128)(2,1)S(1)}, bf16[512,1024]{1,0:T(8,128)(2,1)S(1)}, u32[]{:S(2)}, u32[]{:S(2)}) collective-permute-start(bf16[512,1024]{1,0:T(8,128)(2,1)S(1)} %add_convert_fusion.8), channel_id=1, source_target_pairs={{0,2},{1,3},{2,0},{3,1},{4,6},{5,7},{6,4},{7,5},{8,10},{9,11},{10,... | collective-permute-start | bytes 3145736 | tf_op jit(solution)/shard_map/ppermute | solution.py:72
  387.5 45.4 %collective-permute-start.18 = (bf16[512,1024]{1,0:T(8,128)(2,1)S(1)}, bf16[512,1024]{1,0:T(8,128)(2,1)S(1)}, u32[]{:S(2)}, u32[]{:S(2)}) collective-permute-start(bf16[512,1024]{1,0:T(8,128)(2,1)S(1)} %add_convert_fusion.6), channel_id=1, source_target_pairs={{0,2},{1,3},{2,0},{3,1},{4,6},{5,7},{6,4},{7,5},{8,10},{9,11},{10,... | collective-permute-start | bytes 3145736 | tf_op jit(solution)/shard_map/ppermute | solution.py:72
  412.3 33.5 %collective-permute-start.16 = (bf16[512,1024]{1,0:T(8,128)(2,1)}, bf16[512,1024]{1,0:T(8,128)(2,1)}, u32[]{:S(2)}, u32[]{:S(2)}) collective-permute-start(bf16[512,1024]{1,0:T(8,128)(2,1)} %add_convert_fusion.7), channel_id=1, source_target_pairs={{0,1},{1,0},{2,3},{3,2},{4,5},{5,4},{6,7},{7,6},{8,9},{9,8},{10,11... | collective-permute-start | bytes 3145736 | tf_op jit(solution)/shard_map/ppermute | solution.py:74
  433.4 14.3 %collective-permute-start.19 = (bf16[512,1024]{1,0:T(8,128)(2,1)S(1)}, bf16[512,1024]{1,0:T(8,128)(2,1)}, u32[]{:S(2)}, u32[]{:S(2)}) collective-permute-start(bf16[512,1024]{1,0:T(8,128)(2,1)S(1)} %add_convert_fusion.5), channel_id=1, source_target_pairs={{0,1},{1,0},{2,3},{3,2},{4,5},{5,4},{6,7},{7,6},{8,9},{9,8},{10,11... | collective-permute-start | bytes 3145736 | tf_op jit(solution)/shard_map/ppermute | solution.py:74
  518.7 21.4 %collective-permute-start.20 = (bf16[2,2,256,128]{3,2,1,0:T(8,128)(2,1)S(1)}, bf16[2,2,256,128]{3,2,1,0:T(8,128)(2,1)S(1)}, u32[]{:S(2)}, u32[]{:S(2)}) collective-permute-start(bf16[2,2,256,128]{3,2,1,0:T(8,128)(2,1)S(1)} %fusion.265), channel_id=1, source_target_pairs={{4,0},{5,1},{6,2},{7,3},{12,8},{13,9},{14,10},{15,11},{20,16},{21,... | collective-permute-start | bytes 786440 | tf_op jit(solution)/shard_map/ppermute | solution.py:20
  718.6 8.7 collective-permute-start.21
  741.2 207.0 %reduce-scatter.5.cloned.1.call-start = ((), (), s32[]{:S(2)}) async-start(), calls=%async_computation.5 | async-start | bytes 6193152 | tf_op jit(solution)/shard_map/reduce_scatter | solution.py:367
  753.4 17.7 %collective-permute-start.11 = (bf16[512,1024]{1,0:T(8,128)(2,1)S(1)}, bf16[512,1024]{1,0:T(8,128)(2,1)}, u32[]{:S(2)}, u32[]{:S(2)}) collective-permute-start(bf16[512,1024]{1,0:T(8,128)(2,1)S(1)} %broadcast_select_fusion.14), channel_id=1, source_target_pairs={{0,1},{1,0},{2,3},{3,2},{4,5},{5,4},{6,7},{7,6},{8,9},{9,8},{10,11... | collective-permute-start | bytes 3145736 | tf_op jit(solution)/shard_map/ppermute | solution.py:70
  758.6 16.5 %collective-permute-start.8 = (bf16[512,1024]{1,0:T(8,128)(2,1)}, bf16[512,1024]{1,0:T(8,128)(2,1)S(1)}, u32[]{:S(2)}, u32[]{:S(2)}) collective-permute-start(bf16[512,1024]{1,0:T(8,128)(2,1)} %broadcast_select_fusion.17), channel_id=1, source_target_pairs={{0,1},{1,0},{2,3},{3,2},{4,5},{5,4},{6,7},{7,6},{8,9},{9,8},{10,11... | collective-permute-start | bytes 3145736 | tf_op jit(solution)/shard_map/ppermute | solution.py:70
  773.1 35.8 %collective-permute-start.12 = (bf16[512,1024]{1,0:T(8,128)(2,1)S(1)}, bf16[512,1024]{1,0:T(8,128)(2,1)}, u32[]{:S(2)}, u32[]{:S(2)}) collective-permute-start(bf16[512,1024]{1,0:T(8,128)(2,1)S(1)} %add_convert_fusion.10), channel_id=1, source_target_pairs={{0,2},{1,3},{2,0},{3,1},{4,6},{5,7},{6,4},{7,5},{8,10},{9,11},{10,... | collective-permute-start | bytes 3145736 | tf_op jit(solution)/shard_map/ppermute | solution.py:72
  776.7 45.4 %collective-permute-start.9 = (bf16[512,1024]{1,0:T(8,128)(2,1)}, bf16[512,1024]{1,0:T(8,128)(2,1)}, u32[]{:S(2)}, u32[]{:S(2)}) collective-permute-start(bf16[512,1024]{1,0:T(8,128)(2,1)} %add_convert_fusion.12), channel_id=1, source_target_pairs={{0,2},{1,3},{2,0},{3,1},{4,6},{5,7},{6,4},{7,5},{8,10},{9,11},{10,... | collective-permute-start | bytes 3145736 | tf_op jit(solution)/shard_map/ppermute | solution.py:72
  804.0 6.7 collective-permute-start.25
  808.4 16.7 %collective-permute-start.22 = (bf16[512,1024]{1,0:T(8,128)(2,1)S(1)}, bf16[512,1024]{1,0:T(8,128)(2,1)S(1)}, u32[]{:S(2)}, u32[]{:S(2)}) collective-permute-start(bf16[512,1024]{1,0:T(8,128)(2,1)S(1)} %broadcast_select_fusion.5), channel_id=1, source_target_pairs={{0,1},{1,0},{2,3},{3,2},{4,5},{5,4},{6,7},{7,6},{8,9},{9,8},{10,11... | collective-permute-start | bytes 3145736 | tf_op jit(solution)/shard_map/ppermute | solution.py:70
  810.6 58.7 %collective-permute-start.13 = (bf16[512,1024]{1,0:T(8,128)(2,1)S(1)}, bf16[512,1024]{1,0:T(8,128)(2,1)}, u32[]{:S(2)}, u32[]{:S(2)}) collective-permute-start(bf16[512,1024]{1,0:T(8,128)(2,1)S(1)} %add_convert_fusion.9), channel_id=1, source_target_pairs={{0,1},{1,0},{2,3},{3,2},{4,5},{5,4},{6,7},{7,6},{8,9},{9,8},{10,11... | collective-permute-start | bytes 3145736 | tf_op jit(solution)/shard_map/ppermute | solution.py:74
  812.3 58.4 %collective-permute-start.26 = (bf16[512,1024]{1,0:T(8,128)(2,1)}, bf16[512,1024]{1,0:T(8,128)(2,1)}, u32[]{:S(2)}, u32[]{:S(2)}) collective-permute-start(bf16[512,1024]{1,0:T(8,128)(2,1)} %add_convert_fusion.2), channel_id=1, source_target_pairs={{0,2},{1,3},{2,0},{3,1},{4,6},{5,7},{6,4},{7,5},{8,10},{9,11},{10,... | collective-permute-start | bytes 3145736 | tf_op jit(solution)/shard_map/ppermute | solution.py:72
  825.1 47.6 %collective-permute-start.10 = (bf16[512,1024]{1,0:T(8,128)(2,1)}, bf16[512,1024]{1,0:T(8,128)(2,1)}, u32[]{:S(2)}, u32[]{:S(2)}) collective-permute-start(bf16[512,1024]{1,0:T(8,128)(2,1)} %add_convert_fusion.11), channel_id=1, source_target_pairs={{0,1},{1,0},{2,3},{3,2},{4,5},{5,4},{6,7},{7,6},{8,9},{9,8},{10,11... | collective-permute-start | bytes 3145736 | tf_op jit(solution)/shard_map/ppermute | solution.py:74
  826.7 47.8 %collective-permute-start.23 = (bf16[512,1024]{1,0:T(8,128)(2,1)}, bf16[512,1024]{1,0:T(8,128)(2,1)}, u32[]{:S(2)}, u32[]{:S(2)}) collective-permute-start(bf16[512,1024]{1,0:T(8,128)(2,1)} %add_convert_fusion.4), channel_id=1, source_target_pairs={{0,2},{1,3},{2,0},{3,1},{4,6},{5,7},{6,4},{7,5},{8,10},{9,11},{10,... | collective-permute-start | bytes 3145736 | tf_op jit(solution)/shard_map/ppermute | solution.py:72
  872.6 6.9 collective-permute-start.27
  876.5 3.4 collective-permute-start.24
  (153 other events, 1858.0 us)
Sparse Core Ops, SparseCore 0:
  16.0 65.9 all-gather.2
  103.8 87.6 all-gather.4
  741.3 76.7 reduce-scatter.2
  822.0 105.8 reduce-scatter.4
